TPU v7x, 32 devices: a whole 2x2x4 slice. The times are simulated.
32 devices in a mesh: stream: 8 (over z, x), span: 4 (over y, core).
Axes of the slice: x: 2, y: 2, z: 4, core: 2. Of those that a mesh axis runs over, the one named last changes fastest.
Arguments:
- q_now: float32 [5, 128, 128, 128], P(None, 'stream', 'span'), may hold values from -4 to 4
- q_prev: float32 [5, 128, 128, 128], P(None, 'stream', 'span'), may hold values from -4 to 4
- jacobians: float32 [3, 5, 5], replicated, may hold values from -2.5 to 2.5
- fractions: float32 [3, 32, 1024], P(None, ('stream', 'span')), may hold values from 0 to 0.9
- send_blocks: int32 [32, 1024], P(('stream', 'span')), may hold values from -1 to 8191, as said below
- recv_blocks: int32 [32, 1024], P(('stream', 'span')), may hold values from -1 to 8191, as said below
Outputs:
- q_next: float32 [5, 128, 128, 128], P(None, 'stream', 'span')
Inputs may be any that keep to these rules, and one draw needn't show every extreme that they name: In each row of send_blocks, the 32 slots to one destination hold valid brick indices first and -1 after them; a device sends only to devices whose streamwise rank differs from its own by at most 2, and to the device whose rank differs from its own by 16, which always receives exactly 32 valid slots from it; the busiest receivers get several times the mean. recv_blocks[r, s * 32 + k] is -1 exactly where send_blocks[s, r * 32 + k] is; the valid entries of one row are distinct.
All inputs are finite; a program needn't handle non-finite values.
Results may differ from a plain program's by a relative error of at most 0.0003.
Values sent between devices are 32-bit elements; how exact they have to be, the bound alone decides.
No kernel may reach another device: no remote copies, remote signals or barrier semaphores. Data moves between devices by JAX's collectives and lax.ppermute only.
A program may use at most 192 MiB of HBM per device.

v0:
```python
import jax
import jax.numpy as jnp
from jax import lax
from jax.sharding import PartitionSpec as P

FILTER_WEIGHTS = [1.0, -10.0, 45.0, -120.0, 210.0, -252.0, 210.0, -120.0, 45.0, -10.0, 1.0]
SIGMA = 0.6


def extended(cells, sides, width):
    for axis, dim in sides:
        count = lax.axis_size(axis)
        ends = count - 1
        head = lax.slice_in_dim(cells, 0, width, axis=dim)
        tail = lax.slice_in_dim(cells, cells.shape[dim] - width, cells.shape[dim], axis=dim)
        cells = jnp.concatenate(
            [
                lax.ppermute(tail, axis, [(i, (i + 1) % count) for i in range(ends)]),
                cells,
                lax.ppermute(head, axis, [((i + 1) % count, i) for i in range(ends)]),
            ],
            axis=dim,
        )
    return cells


def to_bricks(fields):
    chans, size_x, size_y, size_z = fields.shape
    split = fields.reshape(chans, size_x // 2, 2, size_y // 2, 2, size_z // 2, 2)
    moved = split.transpose(2, 4, 6, 0, 1, 3, 5)
    return moved.reshape(8 * chans, size_x // 2 * (size_y // 2) * (size_z // 2))


def from_bricks(bricks, chans, size_x, size_y, size_z):
    split = bricks.reshape(2, 2, 2, chans, size_x // 2, size_y // 2, size_z // 2)
    moved = split.transpose(3, 4, 0, 5, 1, 6, 2)
    return moved.reshape(chans, size_x, size_y, size_z)


def interpolate(values, fractions):
    slots = values.shape[1]
    cube = values.reshape(2, 2, 2, 10, slots)
    shift_x = fractions[0]
    shift_y = fractions[1]
    shift_z = fractions[2]
    lower = (1.0 - shift_x) * cube[0] + shift_x * cube[1]
    cube = jnp.stack([lower, cube[1]], 0)
    lower = (1.0 - shift_y) * cube[:, 0] + shift_y * cube[:, 1]
    cube = jnp.stack([lower, cube[:, 1]], 1)
    lower = (1.0 - shift_z) * cube[:, :, 0] + shift_z * cube[:, :, 1]
    cube = jnp.stack([lower, cube[:, :, 1]], 2)
    return cube.reshape(80, slots)


def place(bricks, values, targets):
    total = bricks.shape[1]
    where = jnp.where(targets >= 0, targets, total)
    return bricks.at[:, where].set(values, mode="drop")


def fourth(ext, axis):
    size = ext.shape[axis]

    def part(shift):
        return lax.slice_in_dim(ext, 2 + shift, size - 2 + shift, axis=axis)

    return (8.0 * (part(1) - part(-1)) - (part(2) - part(-2))) / 12.0


def rates(ext, jacobians):
    slope_x = fourth(ext[:, :, 2:-2, 2:-2], 1)
    slope_y = fourth(ext[:, 2:-2, :, 2:-2], 2)
    slope_z = fourth(ext[:, 2:-2, 2:-2, :], 3)
    high = lax.Precision.HIGHEST
    total = jnp.einsum("vw,wxyz->vxyz", jacobians[0], slope_x, precision=high)
    total = total + jnp.einsum("vw,wxyz->vxyz", jacobians[1], slope_y, precision=high)
    total = total + jnp.einsum("vw,wxyz->vxyz", jacobians[2], slope_z, precision=high)
    return -total


def tenth(ext, axis):
    size = ext.shape[axis]
    total = FILTER_WEIGHTS[0] * lax.slice_in_dim(ext, 0, size - 10, axis=axis)
    for offset in range(1, 11):
        total = total + FILTER_WEIGHTS[offset] * lax.slice_in_dim(
            ext, offset, size - 10 + offset, axis=axis
        )
    return total


def smooth(ext):
    along_x = tenth(ext[:, :, 5:-5, 5:-5], 1)
    along_y = tenth(ext[:, 5:-5, :, 5:-5], 2)
    along_z = tenth(ext[:, 5:-5, 5:-5, :], 3)
    centre = ext[:, 5:-5, 5:-5, 5:-5]
    return centre + SIGMA / 1024.0 * (along_x + along_y + along_z)


def pad_radial(field, width):
    return jnp.pad(field, ((0, 0), (0, 0), (0, 0), (width, width)))


def per_device(q_now, q_prev, jacobians, fractions, send_blocks, recv_blocks):
    fields = jnp.concatenate([q_now, q_prev], 0)
    chans, size_x, size_y, size_z = fields.shape
    bricks = to_bricks(fields)
    donors = bricks[:, jnp.maximum(send_blocks.reshape(-1), 0)]
    arrived = lax.all_to_all(donors, ("stream", "span"), split_axis=1, concat_axis=1, tiled=True)
    fresh = interpolate(arrived, fractions.reshape(3, -1))
    bricks = place(bricks, fresh, recv_blocks.reshape(-1))
    fields = from_bricks(bricks, chans, size_x, size_y, size_z)
    current = fields[:5]
    older = fields[5:]
    ext = extended(current, (("stream", 1), ("span", 2)), 2)
    rhs = rates(pad_radial(ext, 2), jacobians)
    pre = (4.0 * current - older + rhs) / 3.0
    widened = extended(pre, (("stream", 1), ("span", 2)), 5)
    return smooth(pad_radial(widened, 5))


def solution(mesh):
    in_specs = (
        P(None, "stream", "span", None),
        P(None, "stream", "span", None),
        P(),
        P(None, ("stream", "span"), None),
        P(("stream", "span"), None),
        P(("stream", "span"), None),
    )
    out_specs = P(None, "stream", "span", None)
    return jax.shard_map(
        per_device, mesh=mesh, in_specs=in_specs, out_specs=out_specs, check_vma=False
    )
```

profile of v0, /device:TPU:3, one launch (start us, length us, event | category | flops | bytes accessed | tf_op | source)
XLA Modules:
  0.0 370.1 jit_solution(1701996225358570834)
XLA Ops:
  2.1 16.8 %copy.34 = f32[10,16,32,128]{0,3,2,1:T(8,128)} copy(f32[10,16,32,128]{3,2,1,0:T(8,128)S(1)} %pad_maximum_fusion.1) | data formatting | bytes 5242880 | tf_op jit(solution)/shard_map/concatenate | solution.py:104
  18.9 43.6 %copy.35 = f32[2,2,2,10,8,16,64]{6,5,4,3,2,1,0:T(8,128)} copy(f32[2,2,2,10,8,16,64]{3,2,6,1,5,0,4:T(2,128)} %bitcast.47) | data formatting | bytes 5242880 | tf_op jit(solution)/shard_map/transpose | solution.py:30
  62.6 4.0 %reshape.123 = f32[80,8192]{1,0:T(8,128)S(1)} reshape(f32[2,2,2,10,8,16,64]{6,5,4,3,2,1,0:T(8,128)} %copy.35) | data formatting | bytes 5242880 | tf_op jit(solution)/shard_map/reshape | solution.py:31
  66.6 3.3 copy.39
  70.0 6.2 %gather_fusion = f32[1024,80]{1,0:T(8,128)} fusion(f32[80,8192]{0,1:T(8,128)} %copy.39, s32[1024]{0:T(1024)S(1)} %broadcast_clamp_fusion), kind=kCustom, calls=%fused_computation | custom fusion | bytes 659456 | tf_op jit(solution)/shard_map/gather | solution.py:107
  76.2 6.4 %all-to-all-start = ((f32[80,32,32]{0,2,1:T(8,128)}), f32[80,32,32]{0,2,1:T(8,128)S(1)}, u32[]{:S(2)}, u32[]{:S(2)}) async-start(f32[80,32,32]{0,2,1:T(8,128)} %bitcast.9), calls=%async_computation | async-start | bytes 1048576 | tf_op jit(solution)/shard_map/all_to_all | solution.py:108
  82.7 14.3 %all-to-all-done = f32[80,32,32]{0,2,1:T(8,128)S(1)} async-done(((f32[80,32,32]{0,2,1:T(8,128)}), f32[80,32,32]{0,2,1:T(8,128)S(1)}, u32[]{:S(2)}, u32[]{:S(2)}) %all-to-all-start) | async-done | bytes 327712 | tf_op jit(solution)/shard_map/all_to_all | solution.py:108
  99.6 7.2 %scatter_fusion = f32[80,8192]{0,1:T(8,128)} fusion(f32[80,8192]{0,1:T(8,128)} %copy.39, s32[1024]{0:T(1024)S(1)} %bitcast.57, f32[1024,80]{1,0:T(8,128)S(1)} %copy.40), kind=kCustom, calls=%fused_computation.1 | custom fusion | bytes 987136 | tf_op jit(solution)/shard_map/scatter | solution.py:58
  106.8 3.7 %copy.41 = f32[80,8192]{1,0:T(8,128)S(1)} copy(f32[80,8192]{0,1:T(8,128)} %scatter_fusion) | data formatting | bytes 5242880 | tf_op jit(solution)/shard_map/scatter | solution.py:58
  110.5 3.7 reshape.126
  114.2 4.6 %fusion.78 = (f32[5,8,2,16,2,64,2]{5,3,1,0,6,4,2:T(8,128)}, f32[5,8,2,16,2,64,2]{5,3,1,0,6,4,2:T(8,128)S(1)}) fusion(f32[10,8,2,16,2,64,2]{5,3,1,0,6,4,2:T(8,128)} %bitcast.49), kind=kLoop, calls=%fused_computation.167 | loop fusion | bytes 5242880 | tf_op jit(solution)/shard_map/slice | solution.py:113
  118.7 34.3 %copy.42 = f32[5,8,2,16,2,64,2]{0,6,5,4,3,2,1:T(2,128)} copy(f32[5,8,2,16,2,64,2]{5,3,1,0,6,4,2:T(8,128)S(1)} %get-tuple-element.12) | data formatting | bytes 2621440 | tf_op jit(solution)/shard_map/slice | solution.py:112
  153.0 7.8 %fusion.77 = (f32[5,2,32,128]{0,3,2,1:T(8,128)}, f32[5,2,32,128]{0,3,2,1:T(8,128)}) fusion(f32[5,16,32,128]{0,3,2,1:T(8,128)} %bitcast.44), kind=kLoop, calls=%fused_computation.166 | loop fusion | bytes 655360 | tf_op jit(solution)/shard_map/slice | solution.py:15
  160.8 2.9 copy.46
  163.7 2.8 collective-permute-start
  166.4 2.9 copy.48
  169.3 3.4 collective-permute-start.1
  172.8 19.6 %copy.47 = f32[5,16,32,128]{3,2,1,0:T(8,128)S(1)} copy(f32[5,16,32,128]{0,3,2,1:T(8,128)} %bitcast.45) | data formatting | bytes 2621440 | tf_op jit(solution)/shard_map/slice | solution.py:112
  192.3 18.6 %copy.43 = f32[5,16,32,128]{3,0,2,1:T(8,128)} copy(f32[5,16,32,128]{0,3,2,1:T(8,128)} %bitcast.46) | data formatting | bytes 2621440 | tf_op jit(solution)/shard_map/slice | solution.py:112
  210.9 40.4 %copy.44 = f32[5,8,2,16,2,64,2]{0,6,5,4,3,2,1:T(2,128)} copy(f32[5,8,2,16,2,64,2]{5,3,1,0,6,4,2:T(8,128)} %get-tuple-element.11) | data formatting | bytes 2621440 | tf_op jit(solution)/shard_map/slice | solution.py:113
  251.3 18.6 %copy.45 = f32[5,16,32,128]{3,0,2,1:T(8,128)} copy(f32[5,16,32,128]{0,3,2,1:T(8,128)} %bitcast.48) | data formatting | bytes 2621440 | tf_op jit(solution)/shard_map/slice | solution.py:113
  269.9 3.4 collective-permute-start.2
  273.4 2.7 collective-permute-start.3
  277.7 3.7 select_maximum_fusion.4
  288.6 4.5 %broadcast_multiply_fusion = (f32[5,16,32,128]{3,0,2,1:T(8,128)S(1)}, f32[5,16,32,128]{3,0,2,1:T(8,128)}) fusion(f32[16,32,128,5]{2,3,1,0:T(8,128)S(1)} %fusion.50, f32[16,32,128,5]{2,3,1,0:T(8,128)S(1)} %fusion.52, f32[1,5,5]{2,0,1:T(1,128)S(1)} %get-tuple-element.28, f32[5,16,32,128]{3,2,1,0:T(8,128)S(1)} %fusion.62, ...), kind=kOutput, calls=%fused_computation.135 | convolution fusion | flops 21954560 | bytes 9175140 | tf_op jit(solution)/shard_map/vw,wxyz->vxyz/dot_general | solution.py:75
  295.2 3.4 collective-permute-start.5
  298.6 15.9 %collective-permute-done.4 = f32[5,5,32,128]{3,2,1,0:T(8,128)S(1)} collective-permute-done((f32[5,5,32,128]{3,2,1,0:T(8,128)S(1)}, f32[5,5,32,128]{3,2,1,0:T(8,128)S(1)}, u32[]{:S(2)}, u32[]{:S(2)}) %collective-permute-start.4) | collective-permute-done | bytes 409632 | tf_op jit(solution)/shard_map/ppermute | solution.py:18
  315.3 3.0 collective-permute-start.6
  323.9 3.7 collective-permute-done.7
  328.6 5.6 %maximum_maximum_fusion = (f32[5,26,37,128]{3,0,2,1:T(8,128)}, f32[5,26,37,128]{3,0,2,1:T(8,128)}) fusion(f32[5,5,32,128]{3,0,2,1:T(8,128)S(1)} %copy.60, f32[5,16,32,128]{3,0,2,1:T(8,128)S(1)} %get-tuple-element.31, f32[5,5,32,128]{3,0,2,1:T(8,128)S(1)} %copy.58, f32[5,26,5,128]{3,0,2,1:T(8,128)} %copy.64, f32[5,26,5,128]{3,0,2,1:T(8,128)} %copy.66), kind=kLoop, calls=%fused_computation.24 | loop fusion | flops 3694080 | bytes 7720960 | tf_op jit(solution)/shard_map/concatenate | solution.py:16
  334.2 10.2 %select_maximum_fusion = f32[5,26,42,138]{3,0,2,1:T(8,128)} fusion(f32[5,26,5,128]{3,0,2,1:T(8,128)} %copy.66, f32[5,26,5,128]{3,0,2,1:T(8,128)} %copy.64, f32[5,5,32,128]{3,0,2,1:T(8,128)S(1)} %copy.60, f32[5,16,32,128]{3,0,2,1:T(8,128)S(1)} %get-tuple-element.31, f32[5,5,32,128]{3,0,2,1:T(8,128)S(1)} %copy.58), kind=kLoop, calls=%fused_computation.4 | loop fusion | flops 9041760 | bytes 5809440 | tf_op jit(solution)/shard_map/concatenate | solution.py:16
  344.4 24.5 %fusion.9 = f32[5,16,32,128]{3,0,2,1:T(8,128)S(1)} fusion(f32[5,16,32,128]{3,0,2,1:T(8,128)S(1)} %get-tuple-element.31, f32[5,5,32,128]{3,0,2,1:T(8,128)S(1)} %copy.60, f32[5,5,32,128]{3,0,2,1:T(8,128)S(1)} %copy.58, f32[5,26,42,138]{3,0,2,1:T(8,128)} %select_maximum_fusion, f32[5,26,37,128]{3,0,2,1:T(8,128)} %get-tuple-element.14, ...), kind=kLoop, calls=%fused_computation.42 | loop fusion | flops 22609920 | bytes 30965760 | tf_op jit(solution)/shard_map/add | solution.py:96
  (58 shorter events, 24.3 us)
Async XLA Ops:
  66.6 3.3 copy-start.4
  70.0 12.7 %copy-start.2 = (f32[3,1,1024]{2,1,0:T(1,128)S(1)}, f32[3,1,1024]{2,1,0:T(1,128)}, u32[]{:S(2)}) copy-start(f32[3,1,1024]{2,1,0:T(1,128)} %param.9) | copy-start | bytes 36868
  70.0 12.8 %copy-start.5 = (s32[1,1024]{1,0:T(1,128)S(1)}, s32[1,1024]{1,0:T(1,128)}, u32[]{:S(2)}) copy-start(s32[1,1024]{1,0:T(1,128)} %param.11) | copy-start | bytes 12292
  76.2 20.9 %all-to-all-start = ((f32[80,32,32]{0,2,1:T(8,128)}), f32[80,32,32]{0,2,1:T(8,128)S(1)}, u32[]{:S(2)}, u32[]{:S(2)}) async-start(f32[80,32,32]{0,2,1:T(8,128)} %bitcast.9), calls=%async_computation | async-start | bytes 1048576 | tf_op jit(solution)/shard_map/all_to_all | solution.py:108
  163.7 106.2 %collective-permute-start = (f32[5,2,32,128]{3,2,1,0:T(8,128)S(1)}, f32[5,2,32,128]{3,2,1,0:T(8,128)S(1)}, u32[]{:S(2)}, u32[]{:S(2)}) collective-permute-start(f32[5,2,32,128]{3,2,1,0:T(8,128)S(1)} %copy.46), channel_id=1, source_target_pairs={{4,0},{8,4},{12,8},{16,12},{20,16},{24,20},{28,24},{5,1},{9,5},{13... | collective-permute-start | bytes 491528 | tf_op jit(solution)/shard_map/ppermute | solution.py:20
  166.4 6.3 %copy-start.3 = (f32[3,5,5]{2,0,1:T(4,128)S(1)}, f32[3,5,5]{2,0,1:T(4,128)}, u32[]{:S(2)}) copy-start(f32[3,5,5]{2,0,1:T(4,128)} %param.8) | copy-start | bytes 904
  169.3 100.5 %collective-permute-start.1 = (f32[5,2,32,128]{3,2,1,0:T(8,128)S(1)}, f32[5,2,32,128]{3,2,1,0:T(8,128)S(1)}, u32[]{:S(2)}, u32[]{:S(2)}) collective-permute-start(f32[5,2,32,128]{3,2,1,0:T(8,128)S(1)} %copy.48), channel_id=1, source_target_pairs={{0,4},{4,8},{8,12},{12,16},{16,20},{20,24},{24,28},{1,5},{5,9},{9,... | collective-permute-start | bytes 491528 | tf_op jit(solution)/shard_map/ppermute | solution.py:18
  269.9 6.5 %collective-permute-start.2 = (f32[5,20,2,128]{3,2,1,0:T(2,128)S(1)}, f32[5,20,2,128]{3,2,1,0:T(2,128)S(1)}, u32[]{:S(2)}, u32[]{:S(2)}) collective-permute-start(f32[5,20,2,128]{3,2,1,0:T(2,128)S(1)} %get-tuple-element.22), channel_id=1, source_target_pairs={{1,0},{2,1},{3,2},{5,4},{6,5},{7,6},{9,8},{10,9},{11,10},{13,12},{... | collective-permute-start | bytes 307208 | tf_op jit(solution)/shard_map/ppermute | solution.py:20
  273.4 4.4 %collective-permute-start.3 = (f32[5,20,2,128]{3,2,1,0:T(2,128)S(1)}, f32[5,20,2,128]{3,2,1,0:T(2,128)S(1)}, u32[]{:S(2)}, u32[]{:S(2)}) collective-permute-start(f32[5,20,2,128]{3,2,1,0:T(2,128)S(1)} %get-tuple-element.21), channel_id=1, source_target_pairs={{0,1},{1,2},{2,3},{4,5},{5,6},{6,7},{8,9},{9,10},{10,11},{12,13},{... | collective-permute-start | bytes 307208 | tf_op jit(solution)/shard_map/ppermute | solution.py:18
  286.0 2.6 copy-start
  286.0 2.6 copy-start.1
  293.2 21.3 %collective-permute-start.4 = (f32[5,5,32,128]{3,2,1,0:T(8,128)S(1)}, f32[5,5,32,128]{3,2,1,0:T(8,128)S(1)}, u32[]{:S(2)}, u32[]{:S(2)}) collective-permute-start(f32[5,5,32,128]{3,2,1,0:T(8,128)S(1)} %copy.57), channel_id=1, source_target_pairs={{0,4},{4,8},{8,12},{12,16},{16,20},{20,24},{24,28},{1,5},{5,9},{9,... | collective-permute-start | bytes 1228808 | tf_op jit(solution)/shard_map/ppermute | solution.py:18
  295.2 19.6 %collective-permute-start.5 = (f32[5,5,32,128]{3,2,1,0:T(8,128)S(1)}, f32[5,5,32,128]{3,2,1,0:T(8,128)S(1)}, u32[]{:S(2)}, u32[]{:S(2)}) collective-permute-start(f32[5,5,32,128]{3,2,1,0:T(8,128)S(1)} %copy.59), channel_id=1, source_target_pairs={{4,0},{8,4},{12,8},{16,12},{20,16},{24,20},{28,24},{5,1},{9,5},{13... | collective-permute-start | bytes 1228808 | tf_op jit(solution)/shard_map/ppermute | solution.py:20
  315.3 7.6 %collective-permute-start.6 = (f32[5,26,5,128]{3,1,2,0:T(8,128)S(1)}, f32[5,26,5,128]{3,1,2,0:T(8,128)S(1)}, u32[]{:S(2)}, u32[]{:S(2)}) collective-permute-start(f32[5,26,5,128]{3,1,2,0:T(8,128)S(1)} %copy.63), channel_id=1, source_target_pairs={{0,1},{1,2},{2,3},{4,5},{5,6},{6,7},{8,9},{9,10},{10,11},{12,13},{... | collective-permute-start | bytes 998408 | tf_op jit(solution)/shard_map/ppermute | solution.py:18
  318.3 9.3 %collective-permute-start.7 = (f32[5,26,5,128]{3,1,2,0:T(8,128)S(1)}, f32[5,26,5,128]{3,1,2,0:T(8,128)S(1)}, u32[]{:S(2)}, u32[]{:S(2)}) collective-permute-start(f32[5,26,5,128]{3,1,2,0:T(8,128)S(1)} %copy.65), channel_id=1, source_target_pairs={{1,0},{2,1},{3,2},{5,4},{6,5},{7,6},{9,8},{10,9},{11,10},{13,12},{... | collective-permute-start | bytes 998408 | tf_op jit(solution)/shard_map/ppermute | solution.py:20
where the time goes:
time: 376 us; the launch traced here: 370 us
  local copies, waits for them, and re-layouts  245 us (65%)
  other arithmetic  48.6 us (13%)
  waiting for transfers between devices  38 us (10%)
  starting transfers between devices  29 us (8%)
  matrix products  9.59 us (3%)
    slice x3, local copies, waits for them, and re-layouts, per_device(): current = fields[:5]  72.4 us
    slice x3, local copies, waits for them, and re-layouts, per_device(): older = fields[5:]  63.5 us
    transpose x1, local copies, waits for them, and re-layouts, to_bricks(): moved = split.transpose(2, 4, 6, 0, 1, 3, 5)  43.6 us
    add x1, other arithmetic, smooth(): return centre + SIGMA / 1024.0 * (along_x + along_y + along_z)  24.5 us
    concatenate x5, other arithmetic, extended(): jnp.concatenate([lax.ppermute(tail, axis, [(i, (i + 1) % count) for i in...  19.9 us
    ppermute x4, waiting for transfers between devices, extended(): lax.ppermute(tail, axis, [(i, (i + 1) % count) for i in range(ends)])  19.8 us
    concatenate x1, local copies, waits for them, and re-layouts, per_device(): fields = jnp.concatenate([q_now, q_prev], 0)  16.8 us
    all_to_all x1, waiting for transfers between devices, per_device(): lax.all_to_all(donors, ('stream', 'span'), split_axis=1, concat_axis=1, t...  14.3 us
  transfers between devices with their start and end apart: 9, of which 6 were waited for; matrix products, arithmetic and copies ran while one was open for 27% of the time, Pallas kernels for 0%

commit v1 on v0

v1 whole, which is shorter than its diff:
```python
import functools

import jax
import jax.numpy as jnp
from jax import lax
from jax.experimental import pallas as pl
from jax.experimental.pallas import tpu as pltpu
from jax.sharding import PartitionSpec as P

TAPS = [-252.0, 210.0, -120.0, 45.0, -10.0, 1.0]
SIGMA = 0.6
REACH = 2
OFFSETS = 2 * REACH + 1
LANES = 128
VMEM_BYTES = 32 * 1024 * 1024
BIG_VMEM_BYTES = 60 * 1024 * 1024
STORE_BYTES = 40 * 1024 * 1024
VMEM = pl.BlockSpec(memory_space=pltpu.VMEM)
SMEM = pl.BlockSpec(memory_space=pltpu.SMEM)
HBM = pl.BlockSpec(memory_space=pltpu.HBM)
ANY = pl.BlockSpec(memory_space=pl.ANY)


def lane_pairs(rows):
    return lax.broadcasted_iota(jnp.int32, (rows, LANES), 1) >> 1


def pack_records(parts):
    lane = lax.broadcasted_iota(jnp.int32, (8, LANES), 1)
    first = jnp.where(lane < 80, parts[0], pltpu.roll(parts[3], 80, 1))
    second = jnp.where(lane < 112, pltpu.roll(parts[3], 32, 1), pltpu.roll(parts[2], 112, 1))
    second = jnp.where(lane < 80, parts[1], second)
    rest = pltpu.roll(parts[2], 112, 1)
    rest = jnp.where(lane < 64, rest, pltpu.roll(pltpu.roll(rest, 4, 0), 64, 1))
    return first[0:4], first[4:8], second[0:4], second[4:8], rest[0:4]


def unpack_records(pieces):
    lane = lax.broadcasted_iota(jnp.int32, (8, LANES), 1)
    first = jnp.concatenate(pieces[0:2], 0)
    second = jnp.concatenate(pieces[2:4], 0)
    rest = jnp.concatenate([pieces[4], pltpu.roll(pieces[4], 64, 1)], 0)
    third = jnp.where(lane < 16, pltpu.roll(second, 16, 1), pltpu.roll(rest, 16, 1))
    fourth = jnp.where(lane < 48, pltpu.roll(first, 48, 1), pltpu.roll(second, 96, 1))
    return first, second, third, fourth


def gather_kernel(
    send_hbm, now_hbm, old_hbm, bricks_hbm, near_hbm,
    fields_ref, bricks_ref, near_ref, turned_ref, stage_ref, send_ref, spot_ref, spots_ref, shelves_ref,
    load_sems, brick_sem, near_sems, table_sems,
    *, streams, spans, slot
):
    chans, size_x, size_y, size_z = now_hbm.shape
    half_y = size_y // 2
    deep = (size_z // 2).bit_length() - 1
    rows = 8 * chans
    columns = size_x // 2 * half_y
    here, across = lax.axis_index("stream"), lax.axis_index("span")

    def chunk(n, bx):
        src = (now_hbm, old_hbm)[n].at[:, pl.ds(2 * bx, 2)]
        dst = fields_ref.at[pl.ds(n * chans, chans), pl.ds(2 * bx, 2), pl.ds(8, size_y)]
        return pltpu.make_async_copy(src, dst, load_sems.at[n, bx])

    table = pltpu.make_async_copy(send_hbm, send_ref, table_sems.at[0])
    table.start()
    for bx in range(size_x // 2):
        chunk(0, bx).start()
        chunk(1, bx).start()
    table.wait()
    pick = jnp.maximum(send_ref[...], 0)
    column = pick >> deep
    group = (column * 171) >> 9
    spot_ref[0:1, :] = group * LANES + 2 * (pick & (size_z // 2 - 1))
    spot_ref[8:9, :] = (column - 3 * group) * LANES
    tables = [
        pltpu.make_async_copy(spot_ref.at[pl.ds(8 * n, 1)], dst, table_sems.at[n + 1])
        for n, dst in enumerate((spots_ref, shelves_ref))
    ]
    for copy in tables:
        copy.start()

    quarter = lax.broadcasted_iota(jnp.int32, (8, LANES), 0) >> 1

    blank = jnp.zeros((LANES - 3 * rows, LANES), jnp.float32)
    turned = 0
    for bx in range(size_x // 2):
        chunk(0, bx).wait()
        chunk(1, bx).wait()
        for by in range(half_y):
            for v in range(rows // 8):
                total = None
                for t in range(4):
                    c, dx = (4 * v + t) // 2, t % 2
                    start = 8 + 2 * by - 2 * t
                    part = fields_ref[c, 2 * bx + dx, start : start + 8, :]
                    total = part if total is None else jnp.where(quarter == t, part, total)
                bricks_ref[bx * half_y + by + 1, 8 * v + 8 : 8 * v + 16, :] = total
        ready = (bx + 1) * half_y
        while 3 * turned < columns and min(3 * turned + 3, columns) <= ready:
            parts = [bricks_ref[min(3 * turned + r + 1, columns), 8 : 8 + rows, :] for r in range(3)]
            turned_ref[turned * LANES : (turned + 1) * LANES, :] = jnp.concatenate([*parts, blank], 0).T
            turned += 1

    keep = pltpu.make_async_copy(bricks_ref, bricks_hbm.at[pl.ds(0, columns + 1)], brick_sem)
    keep.start()

    for copy in tables:
        copy.wait()
    lane = lax.broadcasted_iota(jnp.int32, (8, LANES), 1)

    def fetch(ranks, stage):
        stage[...] = jnp.zeros(stage.shape, jnp.float32)
        for h, rank in enumerate(ranks):
            for k in range(slot):
                spot = spots_ref[0, rank * slot + k]
                shelf = shelves_ref[0, rank * slot + k] + 2 * (slot * h + k)
                stage[pl.ds(shelf, 2), :] = turned_ref[pl.ds(spot, 2), :]
        for h, rank in enumerate(ranks):
            parts = []
            for q in range(4):
                start = 2 * slot * h + 16 * q
                even = [stage[pl.ds(r * LANES + start, 8, stride=2), :] for r in range(3)]
                odd = [stage[pl.ds(r * LANES + start + 1, 8, stride=2), :] for r in range(3)]
                even = even[0] + pltpu.roll(even[1], LANES - rows, 1) + pltpu.roll(even[2], LANES - 2 * rows, 1)
                odd = pltpu.roll(odd[0], rows, 1) + odd[1] + pltpu.roll(odd[2], LANES - rows, 1)
                parts.append(jnp.where(lane < rows, even, odd))
            for q, part in enumerate(pack_records(parts)):
                near_ref[rank, q] = part
            pltpu.make_async_copy(near_ref.at[rank], near_hbm.at[rank], near_sems.at[rank]).start()

    def finish(ranks):
        for rank in ranks:
            pltpu.make_async_copy(near_ref.at[rank], near_hbm.at[rank], near_sems.at[rank]).wait()

    opposite = lax.rem(here + streams // 2, streams) * spans + across
    per_offset = spans // 2

    def ranks_of(n):
        stream = here + (n // per_offset - REACH)
        first = stream * spans + 2 * lax.rem(n, per_offset)
        return jnp.logical_and(stream >= 0, stream < streams), (first, first + 1)

    @pl.loop(0, OFFSETS * per_offset)
    def _(n):
        inside, ranks = ranks_of(n)

        @pl.when(inside)
        def _():
            fetch(ranks, stage_ref.at[n])

    fetch((opposite,), stage_ref.at[OFFSETS * per_offset])

    @pl.loop(0, OFFSETS * per_offset)
    def _(n):
        inside, ranks = ranks_of(n)

        @pl.when(inside)
        def _():
            finish(ranks)

    finish((opposite,))
    keep.wait()


def band(weights, size):
    row = lax.broadcasted_iota(jnp.int32, (size, size), 0)
    col = lax.broadcasted_iota(jnp.int32, (size, size), 1)
    total = jnp.zeros((size, size), jnp.float32)
    for shift, weight in weights.items():
        total = jnp.where(row - col == shift, weight, total)
    return total.astype(jnp.bfloat16)


def along_z(values, matrix):
    high = values.astype(jnp.bfloat16)
    low = (values - high.astype(jnp.float32)).astype(jnp.bfloat16)
    total = jnp.dot(high, matrix, preferred_element_type=jnp.float32)
    return total + jnp.dot(low, matrix, preferred_element_type=jnp.float32)


def mix(jac_ref, d, vectors):
    result = []
    for v in range(len(vectors)):
        total = jac_ref[d, v, 0] * vectors[0]
        for w in range(1, len(vectors)):
            total = total + jac_ref[d, v, w] * vectors[w]
        result.append(total)
    return result


def edge_rows(now_ref, jac_ref, x, size_y):
    chans = now_ref.shape[0]
    tile = lax.broadcasted_iota(jnp.int32, (8, LANES), 0)
    vectors = []
    for c in range(chans):
        low = now_ref[c, x + 2, 8:16, :]
        top = now_ref[c, x + 2, size_y : size_y + 8, :]
        low_a, low_b = pltpu.roll(low, 7, 0), pltpu.roll(low, 6, 0)
        top_a, top_b = pltpu.roll(top, 1, 0), pltpu.roll(top, 2, 0)
        value = jnp.where(tile == 7, 8.0 * low_a - low_b, jnp.where(tile == 6, -low_b, 0.0))
        value = jnp.where(tile == 0, top_b - 8.0 * top_a, jnp.where(tile == 1, top_b, value))
        vectors.append(value)
    return mix(jac_ref, 1, vectors)


def mirrored(p, side, last):
    return p + side * (last - 2 * p)


def stream_sides():
    odd = lax.axis_index("stream") & 1
    return 1 - odd, odd


def span_pick(above, below):
    even = (lax.axis_index("span") & 1) == 0
    return jnp.where(even, above, below), jnp.where(even, below, above)


def edge_planes(now_ref, jac_ref, side, start, stop):
    chans = now_ref.shape[0]
    last = now_ref.shape[1] - 5

    def plane(p):
        return mix(jac_ref, 0, [now_ref[c, mirrored(p, side, last) + 2, 8 + start : 8 + stop, :] for c in range(chans)])

    first, second = plane(0), plane(1)
    sign = (1 - 2 * side).astype(jnp.float32)
    return [sign * (8.0 * first[c] - second[c]) for c in range(chans)], [-sign * first[c] for c in range(chans)]


def contribute(now_ref, jac_ref, side, out_ref):
    chans = now_ref.shape[0]
    size_y = now_ref.shape[2] - 16
    last = now_ref.shape[1] - 5
    planes = edge_planes(now_ref, jac_ref, side, 0, size_y)
    tile = lax.broadcasted_iota(jnp.int32, (8, LANES), 0)
    outer = jnp.logical_or(tile < 2, tile >= 6)
    mixed = [edge_rows(now_ref, jac_ref, mirrored(p, side, last), size_y) for p in range(5)]
    for c in range(chans):
        for p in range(2):
            out_ref[c, p * size_y : (p + 1) * size_y, :] = planes[p][c]
        for t in range(3):
            start = 2 * size_y + 8 * t
            if t < 2:
                second = mixed[2 * t + 1][c]
                second = jnp.where(tile < 4, pltpu.roll(second, 2, 0), pltpu.roll(second, 6, 0))
                out_ref[c, start : start + 8, :] = jnp.where(outer, mixed[2 * t][c], second)
            else:
                out_ref[c, start : start + 8, :] = jnp.where(outer, mixed[2 * t][c], 0.0)


def beyond(block, p, lower):
    if p % 2 == 0:
        return block
    return pltpu.roll(block, 6 if lower else 2, 0)


def cells(bricks_ref, c, dx, column):
    quarter = lax.broadcasted_iota(jnp.int32, (8, LANES), 0) >> 1
    total = None
    for s in range(4):
        start = 8 + 4 * c + 2 * dx - 2 * s
        part = bricks_ref[column + s + 1, pl.ds(start, 8), :]
        total = part if total is None else jnp.where(quarter == s, part, total)
    return total


def scatter_rows(recv_ref, fresh_ref, bricks_ref, first, last, *, streams, spans, slot):
    half_z = LANES // 2
    deep = half_z.bit_length() - 1
    here, across = lax.axis_index("stream"), lax.axis_index("span")
    per_offset = spans // 2
    pairs = lane_pairs(last - first)

    def scatter(unit, rank, count):
        values = fresh_ref[unit, first:last, :]
        for h in range(count):
            for k in range(slot):
                target = recv_ref[0, (rank + h) * slot + k]
                shift = (2 * target - 2 * (slot * h + k)) & (LANES - 1)
                moved = pltpu.roll(values, shift, 1)
                spot = bricks_ref.at[(target >> deep) + 1, pl.ds(8 + first, last - first), :]
                pltpu.store(spot, moved, mask=pairs == (target & (half_z - 1)))

    @pl.loop(0, OFFSETS * per_offset)
    def _(n):
        stream = here - (n // per_offset - REACH)
        rank = stream * spans + 2 * lax.rem(n, per_offset)

        @pl.when(jnp.logical_and(stream >= 0, stream < streams))
        def _():
            some = jnp.maximum(recv_ref[0, rank * slot], recv_ref[0, (rank + 1) * slot]) >= 0

            @pl.when(some)
            def _():
                scatter(n, rank, 2)

    scatter(OFFSETS * per_offset, lax.rem(here + streams // 2, streams) * spans + across, 1)


def fill_kernel(
    recv_hbm, frac_ref, jac_ref, base_hbm, near_ref,
    bricks_ref, fresh_ref, now_ref, first_add_ref, second_add_ref,
    spread_ref, flip_ref, recv_ref, sem, brick_sems,
    *, streams, spans, slot
):
    chans = now_ref.shape[0]
    size_x, size_y, size_z = now_ref.shape[1] - 4, now_ref.shape[2] - 16, now_ref.shape[3]
    half_y = size_y // 2
    rows = 8 * chans
    ranks = streams * spans // 2
    here, across = lax.axis_index("stream"), lax.axis_index("span")
    table = pltpu.make_async_copy(recv_hbm, recv_ref, sem)
    split = -(-rows // 16) * 8
    loads = []
    for n, (start, stop) in enumerate(((0, split), (split, rows))):
        inner = (pl.ds(1, size_x // 2 * half_y), pl.ds(8 + start, stop - start))
        loads.append(pltpu.make_async_copy(base_hbm.at[inner], bricks_ref.at[inner], brick_sems.at[n]))
        loads[n].start()
    table.start()

    source = lax.broadcasted_iota(jnp.int32, (LANES // 2, LANES), 0)
    copies = (source == lane_pairs(LANES // 2)).astype(jnp.float32)
    spread_ref[...] = jnp.dot(
        frac_ref[...], copies, preferred_element_type=jnp.float32, precision=lax.Precision.HIGHEST
    )
    cube = (rows // 8, 8, LANES)
    sub = lax.broadcasted_iota(jnp.int32, cube, 1)
    lane = lax.broadcasted_iota(jnp.int32, cube, 2)

    def interpolated(unit, rank, count, swap):
        flip = flip_ref.at[unit]
        for h in range(count):
            packed = [near_ref[rank + h, q] for q in range(5)]
            for q, part in enumerate(unpack_records(packed)):
                start = 2 * slot * h + 16 * q
                flip[pl.ds(start, 8, stride=2), :] = part
                flip[pl.ds(start + 1, 8, stride=2), :] = pltpu.roll(part, LANES - rows, 1)
        values = flip[...].T[0:rows].reshape(cube)
        shifts = []
        for d in range(3):
            line = spread_ref[pl.ds(d * ranks + (rank >> 1), 1), :]
            if swap:
                line = jnp.where((rank & 1) == 1, pltpu.roll(line, LANES // 2, 1), line)
            shifts.append(line.reshape(1, 1, LANES))
        low = (1.0 - shifts[0]) * values + shifts[0] * pltpu.roll(values, 6, 1)
        values = jnp.where((sub & 2) == 0, low, values)
        low = (1.0 - shifts[1]) * values + shifts[1] * pltpu.roll(values, 7, 1)
        values = jnp.where((sub & 1) == 0, low, values)
        low = (1.0 - shifts[2]) * values + shifts[2] * pltpu.roll(values, LANES - 1, 2)
        values = jnp.where((lane & 1) == 0, low, values)
        fresh_ref[unit] = values.reshape(rows, LANES)

    per_offset = spans // 2
    opposite = lax.rem(here + streams // 2, streams) * spans + across
    for d in range(OFFSETS):
        rank = jnp.clip(here - (d - REACH), 0, streams - 1) * spans
        for m in range(per_offset):
            interpolated(d * per_offset + m, rank + 2 * m, 2, False)
    interpolated(OFFSETS * per_offset, opposite, 1, True)

    table.wait()
    loads[0].wait()
    scatter_rows(recv_ref, fresh_ref, bricks_ref, 0, split, streams=streams, spans=spans, slot=slot)
    loads[1].wait()

    zeros = jnp.zeros((chans, size_y + 16, LANES), jnp.float32)
    for x in (0, 1, size_x + 2, size_x + 3):
        now_ref[:, x] = zeros
    rim = jnp.zeros((8, LANES), jnp.float32)

    @pl.loop(0, size_x // 2)
    def _(bx):
        for c in range(chans):
            for dx in range(2):
                now_ref[c, 2 * bx + dx + 2, 0:8, :] = rim
                for y in range(0, size_y, 8):
                    now_ref[c, 2 * bx + dx + 2, 8 + y : 16 + y, :] = cells(bricks_ref, c, dx, bx * half_y + y // 2)
                now_ref[c, 2 * bx + dx + 2, size_y + 8 : size_y + 16, :] = rim

    for side, add_ref in zip(stream_sides(), (first_add_ref, second_add_ref)):
        contribute(now_ref, jac_ref, side, add_ref)


def plane_pre(jac_ref, now_ref, bricks_ref, slope_ref, x, put):
    chans, size_y = now_ref.shape[0], now_ref.shape[2] - 16

    def part(c, dx, dy):
        return now_ref[c, x + 2 + dx, 8 + dy : 8 + size_y + dy, :]

    totals = []
    for c in range(chans):
        first = (x >> 1) * (size_y // 2)
        old = [cells(bricks_ref, chans + c, x & 1, first + y // 2) for y in range(0, size_y, 8)]
        totals.append(part(c, 0, 0) * (4.0 / 3.0) - jnp.concatenate(old, 0) * (1.0 / 3.0))
    for d in range(3):
        if d == 0:
            vectors = [8.0 * (part(c, 1, 0) - part(c, -1, 0)) - (part(c, 2, 0) - part(c, -2, 0)) for c in range(chans)]
        elif d == 1:
            vectors = [8.0 * (part(c, 0, 1) - part(c, 0, -1)) - (part(c, 0, 2) - part(c, 0, -2)) for c in range(chans)]
        else:
            vectors = [slope_ref[c, x] for c in range(chans)]
        totals = [total + value for total, value in zip(totals, mix(jac_ref, d, vectors))]
    for v in range(chans):
        put(v, totals[v])


def slope_planes(now_ref, slope_ref, start, count):
    chans, size_y = now_ref.shape[0], now_ref.shape[2] - 16
    slopes = band({1: 8.0, -1: -8.0, 2: -1.0, -2: 1.0}, now_ref.shape[3])
    for x in range(start, start + count):
        plane = now_ref[:, x + 2, 8 : 8 + size_y, :].reshape(chans * size_y, LANES)
        slope_ref[:, x] = along_z(plane, slopes).reshape(chans, size_y, LANES)


def edge_kernel(
    recv_hbm, jac_ref, now_ref, bricks_in, fresh_ref, bricks_ref, first_ref, second_ref, slope_ref, recv_ref, sem,
    *, streams, spans, slot
):
    del bricks_in
    table = pltpu.make_async_copy(recv_hbm, recv_ref, sem)
    table.start()
    chans, last = now_ref.shape[0], now_ref.shape[1] - 5
    slope_planes(now_ref, slope_ref, 0, 5)
    slope_planes(now_ref, slope_ref, last - 4, 5)
    table.wait()
    rows = 8 * chans
    split = -(-rows // 16) * 8
    scatter_rows(recv_ref, fresh_ref, bricks_ref, split, rows, streams=streams, spans=spans, slot=slot)
    for side, out_ref in zip(stream_sides(), (first_ref, second_ref)):

        @pl.loop(0, 5)
        def _(p):
            def put(v, value):
                out_ref[p, v] = value

            plane_pre(jac_ref, now_ref, bricks_ref, slope_ref, mirrored(p, side, last), put)


def tie_kernel(first_ref, left_in, right_in, left_ref, right_ref):
    del first_ref, left_in, right_in, left_ref, right_ref


def inner_kernel(
    jac_ref, now_ref, bricks_ref, first_ref, second_ref, first_mine_ref, second_mine_ref, first_add_ref, second_add_ref,
    pre_ref, first_rim_ref, second_rim_ref, slope_ref
):
    chans, size_x, size_y = now_ref.shape[0], now_ref.shape[1] - 4, now_ref.shape[2] - 16
    last = size_x - 1
    tile = lax.broadcasted_iota(jnp.int32, (8, LANES), 0)
    slope_planes(now_ref, slope_ref, 5, size_x - 10)

    def put(x, c, lower, upper):
        first_rim_ref[x, c], second_rim_ref[x, c] = span_pick(upper, lower)

    def put_rows(x, c, low, top, rows_low, rows_top):
        lower = jnp.where(tile == 5, 0.0, jnp.where(tile < 5, low, rows_low))
        upper = jnp.where(tile == 2, 0.0, jnp.where(tile >= 3, top, rows_top))
        put(x, c, lower, upper)

    refs = ((first_ref, first_mine_ref, first_add_ref), (second_ref, second_mine_ref, second_add_ref))
    sides = [(side, *ref) for side, ref in zip(stream_sides(), refs)]
    for side, src_ref, mine_ref, add_ref in sides:
        for c in range(chans):
            for p in range(5):
                low, top = src_ref[p, c, 0:8, :], src_ref[p, c, size_y - 8 : size_y, :]
                if p < 2:
                    low = low + add_ref[c, p * size_y : p * size_y + 8, :]
                    top = top + add_ref[c, (p + 1) * size_y - 8 : (p + 1) * size_y, :]
                start = 2 * size_y + 8 * (p // 2)
                mine = mine_ref[c, start : start + 8, :]
                put_rows(mirrored(p, side, last), c, low, top, beyond(mine, p, False), beyond(mine, p, True))

    for c in range(chans):
        for t in range(3):
            start = 2 * size_y + 8 * t
            blocks = first_add_ref[c, start : start + 8, :], second_add_ref[c, start : start + 8, :]
            left = jnp.where(sides[0][0] == 0, blocks[0], blocks[1])
            right = pltpu.roll(jnp.where(sides[0][0] == 0, blocks[1], blocks[0]), 4, 0)
            put(size_x + t, c, jnp.where(tile >= 4, left, right), jnp.where(tile < 4, left, right))

    @pl.loop(0, size_x - 10)
    def _(n):
        def keep(v, value):
            pre_ref[v, n] = value

        plane_pre(jac_ref, now_ref, bricks_ref, slope_ref, n + 5, keep)
        mixed = edge_rows(now_ref, jac_ref, n + 5, size_y)
        for c in range(chans):
            put_rows(n + 5, c, pre_ref[c, n, 0:8, :], pre_ref[c, n, size_y - 8 : size_y, :], mixed[c], mixed[c])


def radial_band(size_z):
    weights = {0: TAPS[0]}
    for s in range(1, 6):
        weights[s] = weights[-s] = TAPS[s]
    return band(weights, size_z)


def near_filter_kernel(
    pre_ref, first_ref, second_ref, first_add_ref, second_add_ref,
    first_rim_ref, second_rim_ref, first_from_ref, second_from_ref,
    out_ref, low_rows_ref, top_rows_ref, ext_ref, smooth_ref, *, spans
):
    chans, size_x, size_y, size_z = out_ref.shape
    across = lax.axis_index("span")
    last = size_x - 1
    top = size_y + 8
    has_lower = (across > 0).astype(jnp.float32)
    has_upper = (across < spans - 1).astype(jnp.float32)
    tile = lax.broadcasted_iota(jnp.int32, (8, LANES), 0)
    for x in [*range(5), *range(size_x + 5, size_x + 10)]:
        ext_ref[:, x] = jnp.zeros((chans, size_y + 16, LANES), jnp.float32)

    def fold(x, c, plane):
        up, low = span_pick(first_from_ref[x, c], second_from_ref[x, c])
        my_upper, my_lower = span_pick(first_rim_ref[x, c], second_rim_ref[x, c])
        ext_ref[c, x + 5, 16 : top - 8, :] = plane[8 : size_y - 8]
        ext_ref[c, x + 5, 8:16, :] = plane[0:8] + jnp.where(tile < 2, low, 0.0)
        ext_ref[c, x + 5, top - 8 : top, :] = plane[size_y - 8 :] + jnp.where(tile >= 6, up, 0.0)
        mine = has_lower * jnp.where(tile >= 6, my_lower, 0.0)
        ext_ref[c, x + 5, 0:8, :] = jnp.where(tile >= 3, low, 0.0) + mine
        mine = has_upper * jnp.where(tile < 2, my_upper, 0.0)
        ext_ref[c, x + 5, top : top + 8, :] = jnp.where(tile < 5, up, 0.0) + mine

    @pl.loop(0, size_x - 10)
    def _(n):
        for c in range(chans):
            fold(n + 5, c, pre_ref[c, n])

    refs = ((first_ref, first_add_ref), (second_ref, second_add_ref))
    for side, (src_ref, add_ref) in zip(stream_sides(), refs):
        for p in range(5):
            for c in range(chans):
                plane = src_ref[p, c]
                if p < 2:
                    plane = plane + add_ref[c, p * size_y : (p + 1) * size_y, :]
                fold(mirrored(p, side, last), c, plane)

    top_rows_ref[...], low_rows_ref[...] = span_pick(
        first_from_ref[size_x : size_x + 3], second_from_ref[size_x : size_x + 3]
    )
    radial = radial_band(size_z)

    @pl.loop(0, size_x, unroll=4)
    def _(x):
        plane = ext_ref[:, x + 5, 8:top, :].reshape(chans * size_y, LANES)
        smooth_ref[:, x] = along_z(plane, radial).reshape(chans, size_y, LANES)

    @pl.loop(0, size_x)
    def _(x):
        for c in range(chans):
            centre = ext_ref[c, x + 5, 8:top, :]
            total = smooth_ref[c, x] + (2.0 * TAPS[0]) * centre
            for s in range(1, 6):
                ring = ext_ref[c, x + 5 + s, 8:top, :] + ext_ref[c, x + 5 - s, 8:top, :]
                ring = ring + (ext_ref[c, x + 5, 8 + s : top + s, :] + ext_ref[c, x + 5, 8 - s : top - s, :])
                total = total + TAPS[s] * ring
            out_ref[c, x] = centre + (SIGMA / 1024.0) * total


def far_filter_kernel(
    part_ref, first_mine_ref, second_mine_ref, first_from_ref, second_from_ref, low_rows_ref, top_rows_ref,
    out_hbm, out_ref, middle_sem, sems, *, streams
):
    chans, size_x, size_y, _ = part_ref.shape
    tile = lax.broadcasted_iota(jnp.int32, (8, LANES), 0)
    here = lax.axis_index("stream")
    last = size_x - 1
    scale = SIGMA / 1024.0
    middle = pl.ds(5, size_x - 10)
    still = pltpu.make_async_copy(part_ref.at[:, middle], out_hbm.at[:, middle], middle_sem)
    still.start()

    sides = stream_sides()

    def put(n, c):
        planes = pl.ds(sides[n] * (size_x - 5), 5)
        return pltpu.make_async_copy(out_ref.at[c, planes], out_hbm.at[c, planes], sems.at[n, c])

    refs = ((first_mine_ref, first_from_ref), (second_mine_ref, second_from_ref))
    for n, (own_ref, from_ref) in enumerate(refs):
        side = sides[n]
        has = jnp.where(side == 0, here > 0, here < streams - 1).astype(jnp.float32)
        for c in range(chans):
            planes = []
            for p in range(5):
                plane = from_ref[p, c]
                if p < 2:
                    plane = plane + has * own_ref[c, p * size_y : (p + 1) * size_y, :]
                low, top = low_rows_ref[p // 2, c], top_rows_ref[p // 2, c]
                low = jnp.where(side == 1, pltpu.roll(low, 4, 0), low)
                top = jnp.where(side == 1, pltpu.roll(top, 4, 0), top)
                low = jnp.where(tile < 2, beyond(low, p, True), 0.0)
                top = jnp.where(tile >= 6, beyond(top, p, False), 0.0)
                plane = [plane[0:8] + low, plane[8 : size_y - 8], plane[size_y - 8 :] + top]
                planes.append(jnp.concatenate(plane, 0))
            for x in range(5):
                total = TAPS[x + 1] * planes[0]
                for p in range(1, 5 - x):
                    total = total + TAPS[x + 1 + p] * planes[p]
                at = mirrored(x, side, last)
                out_ref[c, at] = part_ref[c, at] + scale * total
            put(n, c).start()
    still.wait()
    for n in range(2):
        for c in range(chans):
            put(n, c).wait()


def params(size=VMEM_BYTES):
    return pltpu.CompilerParams(vmem_limit_bytes=size)


def per_device(q_now, q_prev, jacobians, fractions, send_blocks, recv_blocks):
    streams, spans = lax.axis_size("stream"), lax.axis_size("span")
    chans, size_x, size_y, size_z = q_now.shape
    slots = send_blocks.shape[1]
    slot = slots // (streams * spans)
    rows = 8 * chans
    columns = size_x // 2 * (size_y // 2)
    units = (OFFSETS * spans + 2) // 2
    f32 = jnp.float32
    shape = jax.ShapeDtypeStruct
    bricks = shape((columns + 1, rows + 16, LANES), f32)
    store = shape((STORE_BYTES // (4 * LANES * (rows + 16)), rows + 16, LANES), f32)
    packed = shape((streams * spans, 5, 4, LANES), f32)
    base, near = pl.pallas_call(
        functools.partial(gather_kernel, streams=streams, spans=spans, slot=slot),
        out_shape=[store, packed],
        in_specs=[HBM] * 3,
        out_specs=[HBM] * 2,
        scratch_shapes=[
            pltpu.VMEM((2 * chans, size_x, size_y + 16, LANES), f32),
            pltpu.VMEM(bricks.shape, f32),
            pltpu.VMEM(packed.shape, f32),
            pltpu.VMEM((-(-columns // 3) * LANES, LANES), f32),
            pltpu.VMEM((units, 3 * LANES, LANES), f32),
            pltpu.VMEM((1, slots), jnp.int32),
            pltpu.VMEM((16, slots), jnp.int32),
            pltpu.SMEM((1, slots), jnp.int32),
            pltpu.SMEM((1, slots), jnp.int32),
            pltpu.SemaphoreType.DMA((2, size_x // 2)),
            pltpu.SemaphoreType.DMA,
            pltpu.SemaphoreType.DMA((streams * spans,)),
            pltpu.SemaphoreType.DMA((3,)),
        ],
        compiler_params=params(BIG_VMEM_BYTES),
    )(send_blocks, q_now, q_prev)

    near = lax.all_to_all(near, ("stream", "span"), split_axis=0, concat_axis=0, tiled=True)

    jac = jacobians * (-1.0 / 36.0)
    frac_rows = 3 * streams * spans // 2
    add = shape((chans, 2 * size_y + 24, LANES), f32)
    bricks, fresh, now, first_mine, second_mine = pl.pallas_call(
        functools.partial(fill_kernel, streams=streams, spans=spans, slot=slot),
        out_shape=[
            bricks, shape((units, rows, LANES), f32), shape((chans, size_x + 4, size_y + 16, LANES), f32), add, add
        ],
        in_specs=[HBM, VMEM, SMEM, HBM, VMEM],
        out_specs=[VMEM] * 5,
        scratch_shapes=[
            pltpu.VMEM((frac_rows, LANES), f32),
            pltpu.VMEM((units, LANES, LANES), f32),
            pltpu.SMEM((1, slots), jnp.int32),
            pltpu.SemaphoreType.DMA,
            pltpu.SemaphoreType.DMA((2,)),
        ],
        compiler_params=params(),
    )(recv_blocks, fractions.reshape(frac_rows, LANES // 2), jac, base, near)

    def swaps(count):
        pairs = [[(i, i + 1) for i in range(start, count - 1, 2)] for start in range(2)]
        return [pair + [(b, a) for a, b in pair] for pair in pairs]

    along_stream, along_span = swaps(streams), swaps(spans)
    first_add = lax.ppermute(first_mine, "stream", along_stream[0])
    second_add = lax.ppermute(second_mine, "stream", along_stream[1])
    side = shape((5, chans, size_y, LANES), f32)
    rim = shape((size_x + 3, chans, 8, LANES), f32)
    slope = pltpu.VMEM((chans, size_x, size_y, LANES), f32)
    bricks, first, second = pl.pallas_call(
        functools.partial(edge_kernel, streams=streams, spans=spans, slot=slot),
        out_shape=[shape(bricks.shape, f32), side, side],
        in_specs=[HBM, SMEM] + [VMEM] * 3,
        out_specs=[VMEM] * 3,
        scratch_shapes=[slope, pltpu.SMEM((1, slots), jnp.int32), pltpu.SemaphoreType.DMA],
        input_output_aliases={3: 0},
        compiler_params=params(),
    )(recv_blocks, jac, now, bricks, fresh)
    first, second = pl.pallas_call(
        tie_kernel,
        out_shape=[side, side],
        in_specs=[ANY, VMEM, VMEM],
        out_specs=[VMEM] * 2,
        input_output_aliases={1: 0, 2: 1},
        compiler_params=params(),
    )(first_add, first, second)
    first_from = lax.ppermute(first, "stream", along_stream[0])
    second_from = lax.ppermute(second, "stream", along_stream[1])
    pre, first_rim, second_rim = pl.pallas_call(
        inner_kernel,
        out_shape=[shape((chans, size_x - 10, size_y, LANES), f32), rim, rim],
        in_specs=[SMEM] + [VMEM] * 8,
        out_specs=[VMEM] * 3,
        scratch_shapes=[slope],
        compiler_params=params(),
    )(jac, now, bricks, first, second, first_mine, second_mine, first_add, second_add)
    first_rows = lax.ppermute(first_rim, "span", along_span[0])
    second_rows = lax.ppermute(second_rim, "span", along_span[1])
    rows_shape = shape((3, chans, 8, LANES), f32)
    part, low_rows, top_rows = pl.pallas_call(
        functools.partial(near_filter_kernel, spans=spans),
        out_shape=[shape(q_now.shape, f32), rows_shape, rows_shape],
        in_specs=[VMEM] * 9,
        out_specs=[VMEM] * 3,
        scratch_shapes=[
            pltpu.VMEM((chans, size_x + 10, size_y + 16, LANES), f32),
            pltpu.VMEM(q_now.shape, f32),
        ],
        compiler_params=params(),
    )(pre, first, second, first_add, second_add, first_rim, second_rim, first_rows, second_rows)
    return pl.pallas_call(
        functools.partial(far_filter_kernel, streams=streams),
        out_shape=shape(q_now.shape, f32),
        in_specs=[VMEM] * 7,
        out_specs=HBM,
        scratch_shapes=[
            pltpu.VMEM(q_now.shape, f32),
            pltpu.SemaphoreType.DMA,
            pltpu.SemaphoreType.DMA((2, chans)),
        ],
        compiler_params=params(),
    )(part, first_mine, second_mine, first_from, second_from, low_rows, top_rows)


def solution(mesh):
    in_specs = (
        P(None, "stream", "span", None),
        P(None, "stream", "span", None),
        P(),
        P(None, ("stream", "span"), None),
        P(("stream", "span"), None),
        P(("stream", "span"), None),
    )
    out_specs = P(None, "stream", "span", None)
    return jax.shard_map(
        per_device, mesh=mesh, in_specs=in_specs, out_specs=out_specs, check_vma=False
    )
```

time: 376 us -> 63.8 us (0.17)
  the two profiles are of different devices: /device:TPU:3 before, /device:TPU:16 now
where the time goes in v1:
time: 63.8 us; the launch traced here: 63.6 us
  Pallas kernels  26.4 us (41%)
  waiting for transfers between devices  21.5 us (34%)
  starting transfers between devices  15.4 us (24%)
    ppermute x1, waiting for transfers between devices, per_device(): first_from = lax.ppermute(first, 'stream', along_stream[0])  9.57 us
    all_to_all x1, waiting for transfers between devices, per_device(): lax.all_to_all(near, ('stream', 'span'), split_axis=0, concat_axis=0, til...  9.09 us
    pallas_call x1, Pallas kernels, per_device(): pl.pallas_call(functools.partial(fill_kernel, streams=streams, spans=span...  7.88 us
    pallas_call x1, Pallas kernels, per_device(): pl.pallas_call(functools.partial(gather_kernel, streams=streams, spans=sp...  6.86 us
    pallas_call x1, Pallas kernels, per_device(): pl.pallas_call(functools.partial(edge_kernel, streams=streams, spans=span...  5.59 us
    all_to_all x1, starting transfers between devices, per_device(): lax.all_to_all(near, ('stream', 'span'), split_axis=0, concat_axis=0, til...  4.93 us
    ppermute x1, starting transfers between devices, per_device(): second_add = lax.ppermute(second_mine, 'stream', along_stream[1])  4.85 us
    ppermute x1, starting transfers between devices, per_device(): second_from = lax.ppermute(second, 'stream', along_stream[1])  3.64 us
  transfers between devices with their start and end apart: 7, of which 4 were waited for; matrix products, arithmetic and copies ran while one was open for 0% of the time, Pallas kernels for 17%

profile of v1, /device:TPU:16, one launch (start us, length us, event | category | flops | bytes accessed | tf_op | source)
XLA Modules:
  0.0 63.6 jit_solution(12815218171833786880)
XLA Ops:
  0.0 0.0 copy-start.1
  0.0 0.0 copy-start.2
  0.0 0.0 copy-start
  0.0 6.9 %shard_map.64 = (f32[1462,56,128]{2,1,0:T(8,128)}, f32[32,5,4,128]{3,2,1,0:T(4,128)}) custom-call(s32[1,1024]{1,0:T(1,128)} %send_hbm.1, f32[5,16,32,128]{3,2,1,0:T(8,128)} %now_hbm.1, f32[5,16,32,128]{3,2,1,0:T(8,128)} %old_hbm.1), custom_call_target="tpu_custom_call" | custom-call | tf_op jit(solution)/shard_map/pallas_call | solution.py:631
  6.9 4.9 %all-to-all-start = ((f32[32,5,4,128]{3,2,1,0:T(4,128)}), f32[32,5,4,128]{3,2,1,0:T(4,128)S(1)}, u32[]{:S(2)}, u32[]{:S(2)}) async-start(f32[32,5,4,128]{3,2,1,0:T(4,128)} %get-tuple-element.24), calls=%async_computation | async-start | bytes 655360 | tf_op jit(solution)/shard_map/all_to_all | solution.py:654
  11.8 0.0 copy-done.1
  11.9 0.1 reshape.3.frac_ref
  11.9 0.0 copy-done.2
  12.0 9.1 %all-to-all-done.near_ref = f32[32,5,4,128]{3,2,1,0:T(4,128)S(1)} async-done(((f32[32,5,4,128]{3,2,1,0:T(4,128)}), f32[32,5,4,128]{3,2,1,0:T(4,128)S(1)}, u32[]{:S(2)}, u32[]{:S(2)}) %all-to-all-start) | async-done | bytes 327712 | tf_op jit(solution)/shard_map/all_to_all | solution.py:654
  21.0 0.0 copy-done
  21.1 7.9 %shard_map.65 = (f32[129,56,128]{2,1,0:T(8,128)S(1)}, f32[11,40,128]{2,1,0:T(8,128)S(1)}, f32[5,20,48,128]{3,2,1,0:T(8,128)S(1)}, f32[5,88,128]{2,1,0:T(8,128)S(1)}, f32[5,88,128]{2,1,0:T(8,128)S(1)}) custom-call(s32[1,1024]{1,0:T(1,128)S(1)} %copy-done, f32[48,64]{1,0:T(8,128)S(1)} %reshape.3.frac_ref, f32[3,5,5]{2,1,0:T(8,128)S(1)} %copy_multiply_fusion.jac_ref, ...), custom_call_target="tpu_custom_call" | custom-call | tf_op jit(solution)/shard_map/pallas_call | solution.py:659
  28.9 1.0 %collective-permute-start = (f32[5,88,128]{2,1,0:T(8,128)S(1)}, f32[5,88,128]{2,1,0:T(8,128)S(1)}, u32[]{:S(2)}, u32[]{:S(2)}) collective-permute-start(f32[5,88,128]{2,1,0:T(8,128)S(1)} %get-tuple-element.29.first_mine_ref), channel_id=1, source_target_pairs={{0,4},{8,12},{16,20},{24,28},{4,0},{12,8},{20,16},{28,24},{1,5},{9... | collective-permute-start | bytes 675848 | tf_op jit(solution)/shard_map/ppermute | solution.py:681
  29.9 4.8 %collective-permute-start.1 = (f32[5,88,128]{2,1,0:T(8,128)S(1)}, f32[5,88,128]{2,1,0:T(8,128)S(1)}, u32[]{:S(2)}, u32[]{:S(2)}) collective-permute-start(f32[5,88,128]{2,1,0:T(8,128)S(1)} %get-tuple-element.34.second_mine_ref), channel_id=1, source_target_pairs={{4,8},{12,16},{20,24},{8,4},{16,12},{24,20},{5,9},{13,17},{21,25},... | collective-permute-start | bytes 675848 | tf_op jit(solution)/shard_map/ppermute | solution.py:682
  34.8 5.6 %shard_map.66 = (f32[129,56,128]{2,1,0:T(8,128)S(1)}, f32[5,5,32,128]{3,2,1,0:T(8,128)S(1)}, f32[5,5,32,128]{3,2,1,0:T(8,128)S(1)}) custom-call(s32[1,1024]{1,0:T(1,128)S(1)} %copy-done, f32[3,5,5]{2,1,0:T(8,128)S(1)} %copy_multiply_fusion.jac_ref, f32[5,20,48,128]{3,2,1,0:T(8,128)S(1)} %get-tuple-element.25.now_ref, ...), custom_call_target="tpu_custom_call", output_to_operand_aliasing={{0}: (3, {})} | custom-call | tf_op jit(solution)/shard_map/pallas_call | solution.py:686
  40.4 1.8 %collective-permute-done.first_ref.first_add_ref = f32[5,88,128]{2,1,0:T(8,128)S(1)} collective-permute-done((f32[5,88,128]{2,1,0:T(8,128)S(1)}, f32[5,88,128]{2,1,0:T(8,128)S(1)}, u32[]{:S(2)}, u32[]{:S(2)}) %collective-permute-start) | collective-permute-done | bytes 225312 | tf_op jit(solution)/shard_map/ppermute | solution.py:681
  42.2 0.3 collective-permute-start.4
  42.5 3.6 %collective-permute-start.5 = (f32[5,5,32,128]{3,2,1,0:T(8,128)S(1)}, f32[5,5,32,128]{3,2,1,0:T(8,128)S(1)}, u32[]{:S(2)}, u32[]{:S(2)}) collective-permute-start(f32[5,5,32,128]{3,2,1,0:T(8,128)S(1)} %get-tuple-element.33.second_ref), channel_id=1, source_target_pairs={{4,8},{12,16},{20,24},{8,4},{16,12},{24,20},{5,9},{13,17},{21,25},... | collective-permute-start | bytes 1228808 | tf_op jit(solution)/shard_map/ppermute | solution.py:704
  46.1 0.0 collective-permute-done.1.second_add_ref
  46.2 2.1 %shard_map.68 = (f32[5,6,32,128]{3,2,1,0:T(8,128)S(1)}, f32[19,5,8,128]{3,2,1,0:T(8,128)S(1)}, f32[19,5,8,128]{3,2,1,0:T(8,128)S(1)}) custom-call(f32[3,5,5]{2,1,0:T(8,128)S(1)} %copy_multiply_fusion.jac_ref, f32[5,20,48,128]{3,2,1,0:T(8,128)S(1)} %get-tuple-element.25.now_ref, f32[129,56,128]{2,1,0:T(8,128)S(1)} %get-tuple-element.28.bricks_ref, ...), custom_call_target="tpu_custom_call" | custom-call | tf_op jit(solution)/shard_map/pallas_call | solution.py:705
  48.3 0.1 collective-permute-start.2
  48.4 0.7 %collective-permute-start.3 = (f32[19,5,8,128]{3,2,1,0:T(8,128)S(1)}, f32[19,5,8,128]{3,2,1,0:T(8,128)S(1)}, u32[]{:S(2)}, u32[]{:S(2)}) collective-permute-start(f32[19,5,8,128]{3,2,1,0:T(8,128)S(1)} %get-tuple-element.37.second_rim_ref), channel_id=1, source_target_pairs={{1,2},{2,1},{5,6},{6,5},{9,10},{10,9},{13,14},{14,13},{17,18},{18,... | collective-permute-start | bytes 1167368 | tf_op jit(solution)/shard_map/ppermute | solution.py:714
  49.1 1.0 %collective-permute-done.2.first_from_ref = f32[19,5,8,128]{3,2,1,0:T(8,128)S(1)} collective-permute-done((f32[19,5,8,128]{3,2,1,0:T(8,128)S(1)}, f32[19,5,8,128]{3,2,1,0:T(8,128)S(1)}, u32[]{:S(2)}, u32[]{:S(2)}) %collective-permute-start.2) | collective-permute-done | bytes 389152 | tf_op jit(solution)/shard_map/ppermute | solution.py:713
  50.1 0.0 collective-permute-done.3.second_from_ref
  50.1 2.8 %shard_map.69 = (f32[5,16,32,128]{3,2,1,0:T(8,128)S(1)}, f32[3,5,8,128]{3,2,1,0:T(8,128)S(1)}, f32[3,5,8,128]{3,2,1,0:T(8,128)S(1)}) custom-call(f32[5,6,32,128]{3,2,1,0:T(8,128)S(1)} %get-tuple-element.35.pre_ref, f32[5,5,32,128]{3,2,1,0:T(8,128)S(1)} %get-tuple-element.32.first_ref, f32[5,5,32,128]{3,2,1,0:T(8,128)S(1)} %get-tuple-element.33.second_ref, ...), custom_call_target="tpu_custom_call" | custom-call | tf_op jit(solution)/shard_map/pallas_call | solution.py:716
  52.9 9.6 %collective-permute-done.4.first_from_ref = f32[5,5,32,128]{3,2,1,0:T(8,128)S(1)} collective-permute-done((f32[5,5,32,128]{3,2,1,0:T(8,128)S(1)}, f32[5,5,32,128]{3,2,1,0:T(8,128)S(1)}, u32[]{:S(2)}, u32[]{:S(2)}) %collective-permute-start.4) | collective-permute-done | bytes 409632 | tf_op jit(solution)/shard_map/ppermute | solution.py:703
  62.4 0.0 collective-permute-done.5.second_from_ref
  62.4 1.1 %shard_map.70 = f32[5,16,32,128]{3,2,1,0:T(8,128)} custom-call(f32[5,16,32,128]{3,2,1,0:T(8,128)S(1)} %get-tuple-element.38.part_ref, f32[5,88,128]{2,1,0:T(8,128)S(1)} %get-tuple-element.29.first_mine_ref, f32[5,88,128]{2,1,0:T(8,128)S(1)} %get-tuple-element.34.second_mine_ref, f32[5,5,32,128]{3,2,1,0:T(8,128)S(1)} %collective-permute-done.4.first_from_ref, ...), custom_call_target="tpu_custom_call" | custom-call | tf_op jit(solution)/shard_map/pallas_call | solution.py:727
  (3 shorter events, 0.0 us)
Async XLA Ops:
  0.0 11.8 %copy-start.1 = (f32[3,1,1024]{2,1,0:T(1,128)S(1)}, f32[3,1,1024]{2,1,0:T(1,128)}, u32[]{:S(2)}) copy-start(f32[3,1,1024]{2,1,0:T(1,128)} %param.9) | copy-start | bytes 36868
  0.0 11.9 %copy-start.2 = (f32[3,5,5]{2,0,1:T(4,128)S(1)}, f32[3,5,5]{2,0,1:T(4,128)}, u32[]{:S(2)}) copy-start(f32[3,5,5]{2,0,1:T(4,128)} %param.8) | copy-start | bytes 904
  0.0 21.0 %copy-start = (s32[1,1024]{1,0:T(1,128)S(1)}, s32[1,1024]{1,0:T(1,128)}, u32[]{:S(2)}) copy-start(s32[1,1024]{1,0:T(1,128)} %recv_hbm.3) | copy-start | bytes 12292
  6.9 14.2 %all-to-all-start = ((f32[32,5,4,128]{3,2,1,0:T(4,128)}), f32[32,5,4,128]{3,2,1,0:T(4,128)S(1)}, u32[]{:S(2)}, u32[]{:S(2)}) async-start(f32[32,5,4,128]{3,2,1,0:T(4,128)} %get-tuple-element.24), calls=%async_computation | async-start | bytes 655360 | tf_op jit(solution)/shard_map/all_to_all | solution.py:654
  28.9 13.3 %collective-permute-start = (f32[5,88,128]{2,1,0:T(8,128)S(1)}, f32[5,88,128]{2,1,0:T(8,128)S(1)}, u32[]{:S(2)}, u32[]{:S(2)}) collective-permute-start(f32[5,88,128]{2,1,0:T(8,128)S(1)} %get-tuple-element.29.first_mine_ref), channel_id=1, source_target_pairs={{0,4},{8,12},{16,20},{24,28},{4,0},{12,8},{20,16},{28,24},{1,5},{9... | collective-permute-start | bytes 675848 | tf_op jit(solution)/shard_map/ppermute | solution.py:681
  29.9 16.2 %collective-permute-start.1 = (f32[5,88,128]{2,1,0:T(8,128)S(1)}, f32[5,88,128]{2,1,0:T(8,128)S(1)}, u32[]{:S(2)}, u32[]{:S(2)}) collective-permute-start(f32[5,88,128]{2,1,0:T(8,128)S(1)} %get-tuple-element.34.second_mine_ref), channel_id=1, source_target_pairs={{4,8},{12,16},{20,24},{8,4},{16,12},{24,20},{5,9},{13,17},{21,25},... | collective-permute-start | bytes 675848 | tf_op jit(solution)/shard_map/ppermute | solution.py:682
  42.2 20.2 %collective-permute-start.4 = (f32[5,5,32,128]{3,2,1,0:T(8,128)S(1)}, f32[5,5,32,128]{3,2,1,0:T(8,128)S(1)}, u32[]{:S(2)}, u32[]{:S(2)}) collective-permute-start(f32[5,5,32,128]{3,2,1,0:T(8,128)S(1)} %get-tuple-element.32.first_ref), channel_id=1, source_target_pairs={{0,4},{8,12},{16,20},{24,28},{4,0},{12,8},{20,16},{28,24},{1,5},{9... | collective-permute-start | bytes 1228808 | tf_op jit(solution)/shard_map/ppermute | solution.py:703
  42.5 20.0 %collective-permute-start.5 = (f32[5,5,32,128]{3,2,1,0:T(8,128)S(1)}, f32[5,5,32,128]{3,2,1,0:T(8,128)S(1)}, u32[]{:S(2)}, u32[]{:S(2)}) collective-permute-start(f32[5,5,32,128]{3,2,1,0:T(8,128)S(1)} %get-tuple-element.33.second_ref), channel_id=1, source_target_pairs={{4,8},{12,16},{20,24},{8,4},{16,12},{24,20},{5,9},{13,17},{21,25},... | collective-permute-start | bytes 1228808 | tf_op jit(solution)/shard_map/ppermute | solution.py:704
  48.3 1.8 %collective-permute-start.2 = (f32[19,5,8,128]{3,2,1,0:T(8,128)S(1)}, f32[19,5,8,128]{3,2,1,0:T(8,128)S(1)}, u32[]{:S(2)}, u32[]{:S(2)}) collective-permute-start(f32[19,5,8,128]{3,2,1,0:T(8,128)S(1)} %get-tuple-element.36.first_rim_ref), channel_id=1, source_target_pairs={{0,1},{2,3},{1,0},{3,2},{4,5},{6,7},{5,4},{7,6},{8,9},{10,11},{9,8... | collective-permute-start | bytes 1167368 | tf_op jit(solution)/shard_map/ppermute | solution.py:713
  48.4 1.7 %collective-permute-start.3 = (f32[19,5,8,128]{3,2,1,0:T(8,128)S(1)}, f32[19,5,8,128]{3,2,1,0:T(8,128)S(1)}, u32[]{:S(2)}, u32[]{:S(2)}) collective-permute-start(f32[19,5,8,128]{3,2,1,0:T(8,128)S(1)} %get-tuple-element.37.second_rim_ref), channel_id=1, source_target_pairs={{1,2},{2,1},{5,6},{6,5},{9,10},{10,9},{13,14},{14,13},{17,18},{18,... | collective-permute-start | bytes 1167368 | tf_op jit(solution)/shard_map/ppermute | solution.py:714

commit v2 on v1

--- a/solution.py
+++ b/solution.py
@@ -46,8 +46,8 @@
 
 
 def gather_kernel(
-    send_hbm, now_hbm, old_hbm, bricks_hbm, near_hbm,
-    fields_ref, bricks_ref, near_ref, turned_ref, stage_ref, send_ref, spot_ref, spots_ref, shelves_ref,
+    send_hbm, recv_hbm, now_hbm, old_hbm, bricks_hbm, near_hbm, tables_hbm,
+    fields_ref, bricks_ref, near_ref, turned_ref, stage_ref, send_ref, recv_ref, spot_ref, spots_ref, shelves_ref,
     load_sems, brick_sem, near_sems, table_sems,
     *, streams, spans, slot
 ):
@@ -65,6 +65,8 @@
 
     table = pltpu.make_async_copy(send_hbm, send_ref, table_sems.at[0])
     table.start()
+    received = pltpu.make_async_copy(recv_hbm, recv_ref, table_sems.at[3])
+    received.start()
     for bx in range(size_x // 2):
         chunk(0, bx).start()
         chunk(1, bx).start()
@@ -79,6 +81,17 @@
         for n, dst in enumerate((spots_ref, shelves_ref))
     ]
     for copy in tables:
+        copy.start()
+    received.wait()
+    target = recv_ref[...]
+    slots = lax.broadcasted_iota(jnp.int32, target.shape, 1)
+    spot_ref[16:17, :] = (target >> deep) + 1
+    spot_ref[24:25, :] = (2 * target - 2 * slots) & (LANES - 1)
+    kept = [
+        pltpu.make_async_copy(spot_ref.at[pl.ds(8 * n, 1)], dst, table_sems.at[n + 2])
+        for n, dst in ((2, tables_hbm.at[0]), (3, tables_hbm.at[1]))
+    ]
+    for copy in kept:
         copy.start()
 
     quarter = lax.broadcasted_iota(jnp.int32, (8, LANES), 0) >> 1
@@ -162,6 +175,8 @@
 
     finish((opposite,))
     keep.wait()
+    for copy in kept:
+        copy.wait()
 
 
 def band(weights, size):
@@ -268,22 +283,29 @@
     return total
 
 
-def scatter_rows(recv_ref, fresh_ref, bricks_ref, first, last, *, streams, spans, slot):
-    half_z = LANES // 2
-    deep = half_z.bit_length() - 1
+def load_tables(tables_hbm, tables, sems):
+    copies = [pltpu.make_async_copy(tables_hbm.at[n], dst, sems.at[n]) for n, dst in enumerate(tables)]
+    for copy in copies:
+        copy.start()
+    return copies
+
+
+def scatter_rows(tables, fresh_ref, bricks_ref, first, last, *, streams, spans, slot):
+    columns_ref, shifts_ref = tables
     here, across = lax.axis_index("stream"), lax.axis_index("span")
     per_offset = spans // 2
-    pairs = lane_pairs(last - first)
-
-    def scatter(unit, rank, count):
+    lane = lax.broadcasted_iota(jnp.int32, (last - first, LANES), 1)
+
+    def scatter(unit, rank, count, turn):
         values = fresh_ref[unit, first:last, :]
         for h in range(count):
             for k in range(slot):
-                target = recv_ref[0, (rank + h) * slot + k]
-                shift = (2 * target - 2 * (slot * h + k)) & (LANES - 1)
+                shift = shifts_ref[0, (rank + h) * slot + k]
+                if turn is not None:
+                    shift = (shift + turn) & (LANES - 1)
                 moved = pltpu.roll(values, shift, 1)
-                spot = bricks_ref.at[(target >> deep) + 1, pl.ds(8 + first, last - first), :]
-                pltpu.store(spot, moved, mask=pairs == (target & (half_z - 1)))
+                spot = bricks_ref.at[columns_ref[0, (rank + h) * slot + k], pl.ds(8 + first, last - first), :]
+                pltpu.store(spot, moved, mask=((lane - shift) & (LANES - 2)) == 2 * (slot * h + k))
 
     @pl.loop(0, OFFSETS * per_offset)
     def _(n):
@@ -292,19 +314,20 @@
 
         @pl.when(jnp.logical_and(stream >= 0, stream < streams))
         def _():
-            some = jnp.maximum(recv_ref[0, rank * slot], recv_ref[0, (rank + 1) * slot]) >= 0
+            some = jnp.maximum(columns_ref[0, rank * slot], columns_ref[0, (rank + 1) * slot]) > 0
 
             @pl.when(some)
             def _():
-                scatter(n, rank, 2)
-
-    scatter(OFFSETS * per_offset, lax.rem(here + streams // 2, streams) * spans + across, 1)
+                scatter(n, rank, 2, None)
+
+    opposite = lax.rem(here + streams // 2, streams) * spans + across
+    scatter(OFFSETS * per_offset, opposite, 1, 2 * slot * (opposite & 1))
 
 
 def fill_kernel(
-    recv_hbm, frac_ref, jac_ref, base_hbm, near_ref,
+    tables_hbm, frac_ref, jac_ref, base_hbm, near_ref,
     bricks_ref, fresh_ref, now_ref, first_add_ref, second_add_ref,
-    spread_ref, flip_ref, recv_ref, sem, brick_sems,
+    spread_ref, flip_ref, columns_ref, shifts_ref, table_sems, brick_sems,
     *, streams, spans, slot
 ):
     chans = now_ref.shape[0]
@@ -313,14 +336,14 @@
     rows = 8 * chans
     ranks = streams * spans // 2
     here, across = lax.axis_index("stream"), lax.axis_index("span")
-    table = pltpu.make_async_copy(recv_hbm, recv_ref, sem)
     split = -(-rows // 16) * 8
     loads = []
     for n, (start, stop) in enumerate(((0, split), (split, rows))):
         inner = (pl.ds(1, size_x // 2 * half_y), pl.ds(8 + start, stop - start))
         loads.append(pltpu.make_async_copy(base_hbm.at[inner], bricks_ref.at[inner], brick_sems.at[n]))
         loads[n].start()
-    table.start()
+    tables = (columns_ref, shifts_ref)
+    table_copies = load_tables(tables_hbm, tables, table_sems)
 
     source = lax.broadcasted_iota(jnp.int32, (LANES // 2, LANES), 0)
     copies = (source == lane_pairs(LANES // 2)).astype(jnp.float32)
@@ -331,15 +354,29 @@
     sub = lax.broadcasted_iota(jnp.int32, cube, 1)
     lane = lax.broadcasted_iota(jnp.int32, cube, 2)
 
-    def interpolated(unit, rank, count, swap):
-        flip = flip_ref.at[unit]
-        for h in range(count):
-            packed = [near_ref[rank + h, q] for q in range(5)]
-            for q, part in enumerate(unpack_records(packed)):
+    wide = lax.broadcasted_iota(jnp.int32, (8, LANES), 1)
+
+    def turned(group, members):
+        flip = flip_ref.at[group]
+        for h in range(2):
+            blocks = []
+            for _, rank, count, _ in members:
+                packed = [near_ref[rank + min(h, count - 1), q] for q in range(5)]
+                blocks.append(unpack_records(packed))
+            while len(blocks) < 3:
+                blocks.append(blocks[-1])
+            for q in range(4):
+                a, b, c = (block[q] for block in blocks)
                 start = 2 * slot * h + 16 * q
-                flip[pl.ds(start, 8, stride=2), :] = part
-                flip[pl.ds(start + 1, 8, stride=2), :] = pltpu.roll(part, LANES - rows, 1)
-        values = flip[...].T[0:rows].reshape(cube)
+                even = jnp.where(wide < 2 * rows, pltpu.roll(b, rows, 1), pltpu.roll(c, 2 * rows, 1))
+                flip[pl.ds(start, 8, stride=2), :] = jnp.where(wide < rows, a, even)
+                odd = jnp.where(wide < 2 * rows, b, pltpu.roll(c, rows, 1))
+                flip[pl.ds(start + 1, 8, stride=2), :] = jnp.where(wide < rows, pltpu.roll(a, LANES - rows, 1), odd)
+        block = flip[...].T
+        for n, (unit, rank, _, swap) in enumerate(members):
+            interpolated(unit, rank, swap, block[n * rows : (n + 1) * rows].reshape(cube))
+
+    def interpolated(unit, rank, swap, values):
         shifts = []
         for d in range(3):
             line = spread_ref[pl.ds(d * ranks + (rank >> 1), 1), :]
@@ -356,15 +393,19 @@
 
     per_offset = spans // 2
     opposite = lax.rem(here + streams // 2, streams) * spans + across
+    members = []
     for d in range(OFFSETS):
         rank = jnp.clip(here - (d - REACH), 0, streams - 1) * spans
         for m in range(per_offset):
-            interpolated(d * per_offset + m, rank + 2 * m, 2, False)
-    interpolated(OFFSETS * per_offset, opposite, 1, True)
-
-    table.wait()
+            members.append((d * per_offset + m, rank + 2 * m, 2, False))
+    members.append((OFFSETS * per_offset, opposite, 1, True))
+    for start in range(0, len(members), 3):
+        turned(start // 3, members[start : start + 3])
+
+    for copy in table_copies:
+        copy.wait()
     loads[0].wait()
-    scatter_rows(recv_ref, fresh_ref, bricks_ref, 0, split, streams=streams, spans=spans, slot=slot)
+    scatter_rows(tables, fresh_ref, bricks_ref, 0, split, streams=streams, spans=spans, slot=slot)
     loads[1].wait()
 
     zeros = jnp.zeros((chans, size_y + 16, LANES), jnp.float32)
@@ -417,19 +458,22 @@
 
 
 def edge_kernel(
-    recv_hbm, jac_ref, now_ref, bricks_in, fresh_ref, bricks_ref, first_ref, second_ref, slope_ref, recv_ref, sem,
+    tables_hbm, jac_ref, now_ref, bricks_in, fresh_ref, first_mine_ref, second_mine_ref,
+    bricks_ref, first_ref, second_ref, pre_ref, first_rim_ref, second_rim_ref,
+    slope_ref, columns_ref, shifts_ref, table_sems,
     *, streams, spans, slot
 ):
     del bricks_in
-    table = pltpu.make_async_copy(recv_hbm, recv_ref, sem)
-    table.start()
-    chans, last = now_ref.shape[0], now_ref.shape[1] - 5
-    slope_planes(now_ref, slope_ref, 0, 5)
-    slope_planes(now_ref, slope_ref, last - 4, 5)
-    table.wait()
+    tables = (columns_ref, shifts_ref)
+    copies = load_tables(tables_hbm, tables, table_sems)
+    chans, size_x, size_y = now_ref.shape[0], now_ref.shape[1] - 4, now_ref.shape[2] - 16
+    last = size_x - 1
+    slope_planes(now_ref, slope_ref, 0, size_x)
+    for copy in copies:
+        copy.wait()
     rows = 8 * chans
     split = -(-rows // 16) * 8
-    scatter_rows(recv_ref, fresh_ref, bricks_ref, split, rows, streams=streams, spans=spans, slot=slot)
+    scatter_rows(tables, fresh_ref, bricks_ref, split, rows, streams=streams, spans=spans, slot=slot)
     for side, out_ref in zip(stream_sides(), (first_ref, second_ref)):
 
         @pl.loop(0, 5)
@@ -440,47 +484,21 @@
             plane_pre(jac_ref, now_ref, bricks_ref, slope_ref, mirrored(p, side, last), put)
 
 
-def tie_kernel(first_ref, left_in, right_in, left_ref, right_ref):
-    del first_ref, left_in, right_in, left_ref, right_ref
-
-
-def inner_kernel(
-    jac_ref, now_ref, bricks_ref, first_ref, second_ref, first_mine_ref, second_mine_ref, first_add_ref, second_add_ref,
-    pre_ref, first_rim_ref, second_rim_ref, slope_ref
-):
-    chans, size_x, size_y = now_ref.shape[0], now_ref.shape[1] - 4, now_ref.shape[2] - 16
-    last = size_x - 1
     tile = lax.broadcasted_iota(jnp.int32, (8, LANES), 0)
-    slope_planes(now_ref, slope_ref, 5, size_x - 10)
-
-    def put(x, c, lower, upper):
-        first_rim_ref[x, c], second_rim_ref[x, c] = span_pick(upper, lower)
 
     def put_rows(x, c, low, top, rows_low, rows_top):
         lower = jnp.where(tile == 5, 0.0, jnp.where(tile < 5, low, rows_low))
         upper = jnp.where(tile == 2, 0.0, jnp.where(tile >= 3, top, rows_top))
-        put(x, c, lower, upper)
-
-    refs = ((first_ref, first_mine_ref, first_add_ref), (second_ref, second_mine_ref, second_add_ref))
-    sides = [(side, *ref) for side, ref in zip(stream_sides(), refs)]
-    for side, src_ref, mine_ref, add_ref in sides:
+        first_rim_ref[x, c], second_rim_ref[x, c] = span_pick(upper, lower)
+
+    refs = ((first_ref, first_mine_ref), (second_ref, second_mine_ref))
+    for side, (src_ref, mine_ref) in zip(stream_sides(), refs):
         for c in range(chans):
             for p in range(5):
                 low, top = src_ref[p, c, 0:8, :], src_ref[p, c, size_y - 8 : size_y, :]
-                if p < 2:
-                    low = low + add_ref[c, p * size_y : p * size_y + 8, :]
-                    top = top + add_ref[c, (p + 1) * size_y - 8 : (p + 1) * size_y, :]
                 start = 2 * size_y + 8 * (p // 2)
                 mine = mine_ref[c, start : start + 8, :]
                 put_rows(mirrored(p, side, last), c, low, top, beyond(mine, p, False), beyond(mine, p, True))
-
-    for c in range(chans):
-        for t in range(3):
-            start = 2 * size_y + 8 * t
-            blocks = first_add_ref[c, start : start + 8, :], second_add_ref[c, start : start + 8, :]
-            left = jnp.where(sides[0][0] == 0, blocks[0], blocks[1])
-            right = pltpu.roll(jnp.where(sides[0][0] == 0, blocks[1], blocks[0]), 4, 0)
-            put(size_x + t, c, jnp.where(tile >= 4, left, right), jnp.where(tile < 4, left, right))
 
     @pl.loop(0, size_x - 10)
     def _(n):
@@ -491,6 +509,35 @@
         mixed = edge_rows(now_ref, jac_ref, n + 5, size_y)
         for c in range(chans):
             put_rows(n + 5, c, pre_ref[c, n, 0:8, :], pre_ref[c, n, size_y - 8 : size_y, :], mixed[c], mixed[c])
+
+
+def tie_kernel(add_ref, plane_in, plane_ref):
+    del add_ref, plane_in, plane_ref
+
+
+def relay_kernel(first_add_ref, second_add_ref, first_in, second_in, first_rim_ref, second_rim_ref):
+    del first_in, second_in
+    chans = first_add_ref.shape[0]
+    size_y = (first_add_ref.shape[1] - 24) // 2
+    size_x = first_rim_ref.shape[0] - 3
+    tile = lax.broadcasted_iota(jnp.int32, (8, LANES), 0)
+    sides = stream_sides()
+    for c in range(chans):
+        for side, add_ref in zip(sides, (first_add_ref, second_add_ref)):
+            for p in range(2):
+                x = mirrored(p, side, size_x - 1)
+                lower = jnp.where(tile < 5, add_ref[c, p * size_y : p * size_y + 8, :], 0.0)
+                upper = jnp.where(tile >= 3, add_ref[c, (p + 1) * size_y - 8 : (p + 1) * size_y, :], 0.0)
+                first, second = span_pick(upper, lower)
+                first_rim_ref[x, c] += first
+                second_rim_ref[x, c] += second
+        for t in range(3):
+            start = 2 * size_y + 8 * t
+            blocks = first_add_ref[c, start : start + 8, :], second_add_ref[c, start : start + 8, :]
+            left = jnp.where(sides[0] == 0, blocks[0], blocks[1])
+            right = pltpu.roll(jnp.where(sides[0] == 0, blocks[1], blocks[0]), 4, 0)
+            lower, upper = jnp.where(tile >= 4, left, right), jnp.where(tile < 4, left, right)
+            first_rim_ref[size_x + t, c], second_rim_ref[size_x + t, c] = span_pick(upper, lower)
 
 
 def radial_band(size_z):
@@ -628,11 +675,12 @@
     bricks = shape((columns + 1, rows + 16, LANES), f32)
     store = shape((STORE_BYTES // (4 * LANES * (rows + 16)), rows + 16, LANES), f32)
     packed = shape((streams * spans, 5, 4, LANES), f32)
-    base, near = pl.pallas_call(
+    tables = shape((STORE_BYTES // (4 * slots), 1, slots), jnp.int32)
+    base, near, tables = pl.pallas_call(
         functools.partial(gather_kernel, streams=streams, spans=spans, slot=slot),
-        out_shape=[store, packed],
-        in_specs=[HBM] * 3,
-        out_specs=[HBM] * 2,
+        out_shape=[store, packed, tables],
+        in_specs=[HBM] * 4,
+        out_specs=[HBM] * 3,
         scratch_shapes=[
             pltpu.VMEM((2 * chans, size_x, size_y + 16, LANES), f32),
             pltpu.VMEM(bricks.shape, f32),
@@ -640,16 +688,17 @@
             pltpu.VMEM((-(-columns // 3) * LANES, LANES), f32),
             pltpu.VMEM((units, 3 * LANES, LANES), f32),
             pltpu.VMEM((1, slots), jnp.int32),
-            pltpu.VMEM((16, slots), jnp.int32),
+            pltpu.VMEM((1, slots), jnp.int32),
+            pltpu.VMEM((32, slots), jnp.int32),
             pltpu.SMEM((1, slots), jnp.int32),
             pltpu.SMEM((1, slots), jnp.int32),
             pltpu.SemaphoreType.DMA((2, size_x // 2)),
             pltpu.SemaphoreType.DMA,
             pltpu.SemaphoreType.DMA((streams * spans,)),
-            pltpu.SemaphoreType.DMA((3,)),
+            pltpu.SemaphoreType.DMA((6,)),
         ],
         compiler_params=params(BIG_VMEM_BYTES),
-    )(send_blocks, q_now, q_prev)
+    )(send_blocks, recv_blocks, q_now, q_prev)
 
     near = lax.all_to_all(near, ("stream", "span"), split_axis=0, concat_axis=0, tiled=True)
 
@@ -665,13 +714,14 @@
         out_specs=[VMEM] * 5,
         scratch_shapes=[
             pltpu.VMEM((frac_rows, LANES), f32),
-            pltpu.VMEM((units, LANES, LANES), f32),
+            pltpu.VMEM((-(-units // 3), LANES, LANES), f32),
             pltpu.SMEM((1, slots), jnp.int32),
-            pltpu.SemaphoreType.DMA,
+            pltpu.SMEM((1, slots), jnp.int32),
+            pltpu.SemaphoreType.DMA((2,)),
             pltpu.SemaphoreType.DMA((2,)),
         ],
         compiler_params=params(),
-    )(recv_blocks, fractions.reshape(frac_rows, LANES // 2), jac, base, near)
+    )(tables, fractions.reshape(frac_rows, LANES // 2), jac, base, near)
 
     def swaps(count):
         pairs = [[(i, i + 1) for i in range(start, count - 1, 2)] for start in range(2)]
@@ -682,34 +732,40 @@
     second_add = lax.ppermute(second_mine, "stream", along_stream[1])
     side = shape((5, chans, size_y, LANES), f32)
     rim = shape((size_x + 3, chans, 8, LANES), f32)
-    slope = pltpu.VMEM((chans, size_x, size_y, LANES), f32)
-    bricks, first, second = pl.pallas_call(
+    _, first, second, pre, first_rim, second_rim = pl.pallas_call(
         functools.partial(edge_kernel, streams=streams, spans=spans, slot=slot),
-        out_shape=[shape(bricks.shape, f32), side, side],
-        in_specs=[HBM, SMEM] + [VMEM] * 3,
-        out_specs=[VMEM] * 3,
-        scratch_shapes=[slope, pltpu.SMEM((1, slots), jnp.int32), pltpu.SemaphoreType.DMA],
+        out_shape=[
+            shape(bricks.shape, f32), side, side, shape((chans, size_x - 10, size_y, LANES), f32), rim, rim
+        ],
+        in_specs=[HBM, SMEM] + [VMEM] * 5,
+        out_specs=[VMEM] * 6,
+        scratch_shapes=[
+            pltpu.VMEM((chans, size_x, size_y, LANES), f32),
+            pltpu.SMEM((1, slots), jnp.int32),
+            pltpu.SMEM((1, slots), jnp.int32),
+            pltpu.SemaphoreType.DMA((2,)),
+        ],
         input_output_aliases={3: 0},
         compiler_params=params(),
-    )(recv_blocks, jac, now, bricks, fresh)
-    first, second = pl.pallas_call(
+    )(tables, jac, now, bricks, fresh, first_mine, second_mine)
+    second = pl.pallas_call(
         tie_kernel,
-        out_shape=[side, side],
-        in_specs=[ANY, VMEM, VMEM],
-        out_specs=[VMEM] * 2,
-        input_output_aliases={1: 0, 2: 1},
+        out_shape=side,
+        in_specs=[ANY, VMEM],
+        out_specs=VMEM,
+        input_output_aliases={1: 0},
         compiler_params=params(),
-    )(first_add, first, second)
+    )(first_add, second)
     first_from = lax.ppermute(first, "stream", along_stream[0])
     second_from = lax.ppermute(second, "stream", along_stream[1])
-    pre, first_rim, second_rim = pl.pallas_call(
-        inner_kernel,
-        out_shape=[shape((chans, size_x - 10, size_y, LANES), f32), rim, rim],
-        in_specs=[SMEM] + [VMEM] * 8,
-        out_specs=[VMEM] * 3,
-        scratch_shapes=[slope],
+    first_rim, second_rim = pl.pallas_call(
+        relay_kernel,
+        out_shape=[rim, rim],
+        in_specs=[VMEM] * 4,
+        out_specs=[VMEM] * 2,
+        input_output_aliases={2: 0, 3: 1},
         compiler_params=params(),
-    )(jac, now, bricks, first, second, first_mine, second_mine, first_add, second_add)
+    )(first_add, second_add, first_rim, second_rim)
     first_rows = lax.ppermute(first_rim, "span", along_span[0])
     second_rows = lax.ppermute(second_rim, "span", along_span[1])
     rows_shape = shape((3, chans, 8, LANES), f32)

time: 63.8 us -> 62 us (0.972)
  the two profiles are of different devices: /device:TPU:16 before, /device:TPU:0 now
where the time goes in v2:
time: 62 us; the launch traced here: 61.6 us
  waiting for transfers between devices  24.6 us (40%)
  Pallas kernels  21.5 us (35%)
  starting transfers between devices  15.3 us (25%)
    all_to_all x1, waiting for transfers between devices, per_device(): lax.all_to_all(near, ('stream', 'span'), split_axis=0, concat_axis=0, til...  11.8 us
    ppermute x1, waiting for transfers between devices, per_device(): first_from = lax.ppermute(first, 'stream', along_stream[0])  11.7 us
    all_to_all x1, starting transfers between devices, per_device(): lax.all_to_all(near, ('stream', 'span'), split_axis=0, concat_axis=0, til...  7.42 us
    pallas_call x1, Pallas kernels, per_device(): pl.pallas_call(functools.partial(edge_kernel, streams=streams, spans=span...  5.98 us
    pallas_call x1, Pallas kernels, per_device(): pl.pallas_call(functools.partial(fill_kernel, streams=streams, spans=span...  5.8 us
    pallas_call x1, Pallas kernels, per_device(): pl.pallas_call(functools.partial(gather_kernel, streams=streams, spans=sp...  5.76 us
    ppermute x1, starting transfers between devices, per_device(): first_from = lax.ppermute(first, 'stream', along_stream[0])  4.36 us
    pallas_call x1, Pallas kernels, per_device(): pl.pallas_call(functools.partial(near_filter_kernel, spans=spans), out_sh...  2.77 us
  transfers between devices with their start and end apart: 7, of which 3 were waited for; matrix products, arithmetic and copies ran while one was open for 0% of the time, Pallas kernels for 14%

profile of v2, /device:TPU:0, one launch (start us, length us, event | category | flops | bytes accessed | tf_op | source)
XLA Modules:
  0.0 61.6 jit_solution(11281760665061590156)
XLA Ops:
  0.0 0.0 copy-start
  0.0 0.0 copy-start.1
  0.0 5.8 %shard_map.64 = (f32[1462,56,128]{2,1,0:T(8,128)}, f32[32,5,4,128]{3,2,1,0:T(4,128)}, s32[10240,1,1024]{2,1,0:T(1,128)}) custom-call(s32[1,1024]{1,0:T(1,128)} %send_hbm.1, s32[1,1024]{1,0:T(1,128)} %recv_hbm.1, f32[5,16,32,128]{3,2,1,0:T(8,128)} %now_hbm.1, f32[5,16,32,128]{3,2,1,0:T(8,128)} %old_hbm.1), custom_call_target="tpu_custom_call" | custom-call | tf_op jit(solution)/shard_map/pallas_call | solution.py:679
  5.8 7.4 %all-to-all-start = ((f32[32,5,4,128]{3,2,1,0:T(4,128)}), f32[32,5,4,128]{3,2,1,0:T(4,128)S(1)}, u32[]{:S(2)}, u32[]{:S(2)}) async-start(f32[32,5,4,128]{3,2,1,0:T(4,128)} %get-tuple-element.25), calls=%async_computation | async-start | bytes 655360 | tf_op jit(solution)/shard_map/all_to_all | solution.py:703
  13.2 0.0 copy-done
  13.3 0.1 reshape.3.frac_ref
  13.3 0.0 copy-done.1
  13.3 11.8 %all-to-all-done.near_ref = f32[32,5,4,128]{3,2,1,0:T(4,128)S(1)} async-done(((f32[32,5,4,128]{3,2,1,0:T(4,128)}), f32[32,5,4,128]{3,2,1,0:T(4,128)S(1)}, u32[]{:S(2)}, u32[]{:S(2)}) %all-to-all-start) | async-done | bytes 327712 | tf_op jit(solution)/shard_map/all_to_all | solution.py:703
  25.2 5.8 %shard_map.65 = (f32[129,56,128]{2,1,0:T(8,128)S(1)}, f32[11,40,128]{2,1,0:T(8,128)S(1)}, f32[5,20,48,128]{3,2,1,0:T(8,128)S(1)}, f32[5,88,128]{2,1,0:T(8,128)S(1)}, f32[5,88,128]{2,1,0:T(8,128)S(1)}) custom-call(s32[10240,1,1024]{2,1,0:T(1,128)} %get-tuple-element.23.tables_hbm, f32[48,64]{1,0:T(8,128)S(1)} %reshape.3.frac_ref, ...), custom_call_target="tpu_custom_call" | custom-call | tf_op jit(solution)/shard_map/pallas_call | solution.py:708
  31.0 1.4 %collective-permute-start = (f32[5,88,128]{2,1,0:T(8,128)S(1)}, f32[5,88,128]{2,1,0:T(8,128)S(1)}, u32[]{:S(2)}, u32[]{:S(2)}) collective-permute-start(f32[5,88,128]{2,1,0:T(8,128)S(1)} %get-tuple-element.29.first_mine_ref), channel_id=1, source_target_pairs={{0,4},{8,12},{16,20},{24,28},{4,0},{12,8},{20,16},{28,24},{1,5},{9... | collective-permute-start | bytes 675848 | tf_op jit(solution)/shard_map/ppermute | solution.py:731
  32.4 0.7 %collective-permute-start.1 = (f32[5,88,128]{2,1,0:T(8,128)S(1)}, f32[5,88,128]{2,1,0:T(8,128)S(1)}, u32[]{:S(2)}, u32[]{:S(2)}) collective-permute-start(f32[5,88,128]{2,1,0:T(8,128)S(1)} %get-tuple-element.30.second_mine_ref), channel_id=1, source_target_pairs={{4,8},{12,16},{20,24},{8,4},{16,12},{24,20},{5,9},{13,17},{21,25},... | collective-permute-start | bytes 675848 | tf_op jit(solution)/shard_map/ppermute | solution.py:732
  33.1 6.0 %shard_map.66 = (f32[129,56,128]{2,1,0:T(8,128)S(1)}, f32[5,5,32,128]{3,2,1,0:T(8,128)S(1)}, f32[5,5,32,128]{3,2,1,0:T(8,128)S(1)}, f32[5,6,32,128]{3,2,1,0:T(8,...) custom-call(s32[10240,1,1024]{2,1,0:T(1,128)} %get-tuple-element.23.tables, ...), custom_call_target="tpu_custom_call", output_to_operand_aliasing={{0}: (3, {})} | custom-call | tf_op jit(solution)/shard_map/pallas_call | solution.py:735
  39.1 4.4 %collective-permute-start.4 = (f32[5,5,32,128]{3,2,1,0:T(8,128)S(1)}, f32[5,5,32,128]{3,2,1,0:T(8,128)S(1)}, u32[]{:S(2)}, u32[]{:S(2)}) collective-permute-start(f32[5,5,32,128]{3,2,1,0:T(8,128)S(1)} %get-tuple-element.32.first_ref), channel_id=1, source_target_pairs={{0,4},{8,12},{16,20},{24,28},{4,0},{12,8},{20,16},{28,24},{1,5},{9... | collective-permute-start | bytes 1228808 | tf_op jit(solution)/shard_map/ppermute | solution.py:759
  43.5 0.0 collective-permute-done.add_ref.first_add_ref
  43.5 0.7 %collective-permute-start.5 = (f32[5,5,32,128]{3,2,1,0:T(8,128)S(1)}, f32[5,5,32,128]{3,2,1,0:T(8,128)S(1)}, u32[]{:S(2)}, u32[]{:S(2)}) collective-permute-start(f32[5,5,32,128]{3,2,1,0:T(8,128)S(1)} %shard_map.67.second_ref), channel_id=1, source_target_pairs={{4,8},{12,16},{20,24},{8,4},{16,12},{24,20},{5,9},{13,17},{21,25},... | collective-permute-start | bytes 1228808 | tf_op jit(solution)/shard_map/ppermute | solution.py:760
  44.2 0.0 collective-permute-done.1.second_add_ref
  44.2 0.1 shard_map.68
  44.2 0.1 collective-permute-start.2
  44.3 0.7 %collective-permute-start.3 = (f32[19,5,8,128]{3,2,1,0:T(8,128)S(1)}, f32[19,5,8,128]{3,2,1,0:T(8,128)S(1)}, u32[]{:S(2)}, u32[]{:S(2)}) collective-permute-start(f32[19,5,8,128]{3,2,1,0:T(8,128)S(1)} %get-tuple-element.37.second_rim_ref), channel_id=1, source_target_pairs={{1,2},{2,1},{5,6},{6,5},{9,10},{10,9},{13,14},{14,13},{17,18},{18,... | collective-permute-start | bytes 1167368 | tf_op jit(solution)/shard_map/ppermute | solution.py:770
  45.0 1.0 %collective-permute-done.2.first_from_ref = f32[19,5,8,128]{3,2,1,0:T(8,128)S(1)} collective-permute-done((f32[19,5,8,128]{3,2,1,0:T(8,128)S(1)}, f32[19,5,8,128]{3,2,1,0:T(8,128)S(1)}, u32[]{:S(2)}, u32[]{:S(2)}) %collective-permute-start.2) | collective-permute-done | bytes 389152 | tf_op jit(solution)/shard_map/ppermute | solution.py:769
  46.0 0.0 collective-permute-done.3.second_from_ref
  46.0 2.8 %shard_map.69 = (f32[5,16,32,128]{3,2,1,0:T(8,128)S(1)}, f32[3,5,8,128]{3,2,1,0:T(8,128)S(1)}, f32[3,5,8,128]{3,2,1,0:T(8,128)S(1)}) custom-call(f32[5,6,32,128]{3,2,1,0:T(8,128)S(1)} %get-tuple-element.31.pre_ref, f32[5,5,32,128]{3,2,1,0:T(8,128)S(1)} %get-tuple-element.32.first_ref, f32[5,5,32,128]{3,2,1,0:T(8,128)S(1)} %shard_map.67.second_ref, ...), custom_call_target="tpu_custom_call" | custom-call | tf_op jit(solution)/shard_map/pallas_call | solution.py:772
  48.8 11.7 %collective-permute-done.4.first_from_ref = f32[5,5,32,128]{3,2,1,0:T(8,128)S(1)} collective-permute-done((f32[5,5,32,128]{3,2,1,0:T(8,128)S(1)}, f32[5,5,32,128]{3,2,1,0:T(8,128)S(1)}, u32[]{:S(2)}, u32[]{:S(2)}) %collective-permute-start.4) | collective-permute-done | bytes 409632 | tf_op jit(solution)/shard_map/ppermute | solution.py:759
  60.5 0.0 collective-permute-done.5.second_from_ref
  60.5 1.1 %shard_map.70 = f32[5,16,32,128]{3,2,1,0:T(8,128)} custom-call(f32[5,16,32,128]{3,2,1,0:T(8,128)S(1)} %get-tuple-element.38.part_ref, f32[5,88,128]{2,1,0:T(8,128)S(1)} %get-tuple-element.29.first_mine_ref, f32[5,88,128]{2,1,0:T(8,128)S(1)} %get-tuple-element.30.second_mine_ref, f32[5,5,32,128]{3,2,1,0:T(8,128)S(1)} %collective-permute-done.4.first_from_ref, ...), custom_call_target="tpu_custom_call" | custom-call | tf_op jit(solution)/shard_map/pallas_call | solution.py:783
  (3 shorter events, 0.0 us)
Async XLA Ops:
  0.0 13.2 %copy-start = (f32[3,1,1024]{2,1,0:T(1,128)S(1)}, f32[3,1,1024]{2,1,0:T(1,128)}, u32[]{:S(2)}) copy-start(f32[3,1,1024]{2,1,0:T(1,128)} %param.9) | copy-start | bytes 36868
  0.0 13.3 %copy-start.1 = (f32[3,5,5]{2,0,1:T(4,128)S(1)}, f32[3,5,5]{2,0,1:T(4,128)}, u32[]{:S(2)}) copy-start(f32[3,5,5]{2,0,1:T(4,128)} %param.8) | copy-start | bytes 904
  5.8 19.4 %all-to-all-start = ((f32[32,5,4,128]{3,2,1,0:T(4,128)}), f32[32,5,4,128]{3,2,1,0:T(4,128)S(1)}, u32[]{:S(2)}, u32[]{:S(2)}) async-start(f32[32,5,4,128]{3,2,1,0:T(4,128)} %get-tuple-element.25), calls=%async_computation | async-start | bytes 655360 | tf_op jit(solution)/shard_map/all_to_all | solution.py:703
  31.0 12.5 %collective-permute-start = (f32[5,88,128]{2,1,0:T(8,128)S(1)}, f32[5,88,128]{2,1,0:T(8,128)S(1)}, u32[]{:S(2)}, u32[]{:S(2)}) collective-permute-start(f32[5,88,128]{2,1,0:T(8,128)S(1)} %get-tuple-element.29.first_mine_ref), channel_id=1, source_target_pairs={{0,4},{8,12},{16,20},{24,28},{4,0},{12,8},{20,16},{28,24},{1,5},{9... | collective-permute-start | bytes 675848 | tf_op jit(solution)/shard_map/ppermute | solution.py:731
  32.4 11.7 %collective-permute-start.1 = (f32[5,88,128]{2,1,0:T(8,128)S(1)}, f32[5,88,128]{2,1,0:T(8,128)S(1)}, u32[]{:S(2)}, u32[]{:S(2)}) collective-permute-start(f32[5,88,128]{2,1,0:T(8,128)S(1)} %get-tuple-element.30.second_mine_ref), channel_id=1, source_target_pairs={{4,8},{12,16},{20,24},{8,4},{16,12},{24,20},{5,9},{13,17},{21,25},... | collective-permute-start | bytes 675848 | tf_op jit(solution)/shard_map/ppermute | solution.py:732
  39.1 21.4 %collective-permute-start.4 = (f32[5,5,32,128]{3,2,1,0:T(8,128)S(1)}, f32[5,5,32,128]{3,2,1,0:T(8,128)S(1)}, u32[]{:S(2)}, u32[]{:S(2)}) collective-permute-start(f32[5,5,32,128]{3,2,1,0:T(8,128)S(1)} %get-tuple-element.32.first_ref), channel_id=1, source_target_pairs={{0,4},{8,12},{16,20},{24,28},{4,0},{12,8},{20,16},{28,24},{1,5},{9... | collective-permute-start | bytes 1228808 | tf_op jit(solution)/shard_map/ppermute | solution.py:759
  43.5 17.0 %collective-permute-start.5 = (f32[5,5,32,128]{3,2,1,0:T(8,128)S(1)}, f32[5,5,32,128]{3,2,1,0:T(8,128)S(1)}, u32[]{:S(2)}, u32[]{:S(2)}) collective-permute-start(f32[5,5,32,128]{3,2,1,0:T(8,128)S(1)} %shard_map.67.second_ref), channel_id=1, source_target_pairs={{4,8},{12,16},{20,24},{8,4},{16,12},{24,20},{5,9},{13,17},{21,25},... | collective-permute-start | bytes 1228808 | tf_op jit(solution)/shard_map/ppermute | solution.py:760
  44.2 1.8 %collective-permute-start.2 = (f32[19,5,8,128]{3,2,1,0:T(8,128)S(1)}, f32[19,5,8,128]{3,2,1,0:T(8,128)S(1)}, u32[]{:S(2)}, u32[]{:S(2)}) collective-permute-start(f32[19,5,8,128]{3,2,1,0:T(8,128)S(1)} %get-tuple-element.36.first_rim_ref), channel_id=1, source_target_pairs={{0,1},{2,3},{1,0},{3,2},{4,5},{6,7},{5,4},{7,6},{8,9},{10,11},{9,8... | collective-permute-start | bytes 1167368 | tf_op jit(solution)/shard_map/ppermute | solution.py:769
  44.3 1.7 %collective-permute-start.3 = (f32[19,5,8,128]{3,2,1,0:T(8,128)S(1)}, f32[19,5,8,128]{3,2,1,0:T(8,128)S(1)}, u32[]{:S(2)}, u32[]{:S(2)}) collective-permute-start(f32[19,5,8,128]{3,2,1,0:T(8,128)S(1)} %get-tuple-element.37.second_rim_ref), channel_id=1, source_target_pairs={{1,2},{2,1},{5,6},{6,5},{9,10},{10,9},{13,14},{14,13},{17,18},{18,... | collective-permute-start | bytes 1167368 | tf_op jit(solution)/shard_map/ppermute | solution.py:770

commit v3 on v2

--- a/solution.py
+++ b/solution.py
@@ -324,6 +324,21 @@
     scatter(OFFSETS * per_offset, opposite, 1, 2 * slot * (opposite & 1))
 
 
+def outer_tiles(size_x, size_y):
+    half = size_x // 2
+    every = list(range(0, size_y, 8))
+    ends = [0, size_y - 8]
+    return [(0, every), (half - 1, every)] + [(bx, ends) for bx in (1, 2, half - 3, half - 2)]
+
+
+def lay_out(bricks_ref, now_ref, bx, tiles):
+    half_y = (now_ref.shape[2] - 16) // 2
+    for c in range(now_ref.shape[0]):
+        for dx in range(2):
+            for y in tiles:
+                now_ref[c, 2 * bx + dx + 2, 8 + y : 16 + y, :] = cells(bricks_ref, c, dx, bx * half_y + y // 2)
+
+
 def fill_kernel(
     tables_hbm, frac_ref, jac_ref, base_hbm, near_ref,
     bricks_ref, fresh_ref, now_ref, first_add_ref, second_add_ref,
@@ -337,11 +352,13 @@
     ranks = streams * spans // 2
     here, across = lax.axis_index("stream"), lax.axis_index("span")
     split = -(-rows // 16) * 8
+    quarter = size_x // 2 * half_y // 4
     loads = []
     for n, (start, stop) in enumerate(((0, split), (split, rows))):
-        inner = (pl.ds(1, size_x // 2 * half_y), pl.ds(8 + start, stop - start))
-        loads.append(pltpu.make_async_copy(base_hbm.at[inner], bricks_ref.at[inner], brick_sems.at[n]))
-        loads[n].start()
+        for m in range(4):
+            inner = (pl.ds(1 + m * quarter, quarter), pl.ds(8 + start, stop - start))
+            loads.append(pltpu.make_async_copy(base_hbm.at[inner], bricks_ref.at[inner], brick_sems.at[4 * n + m]))
+            loads[-1].start()
     tables = (columns_ref, shifts_ref)
     table_copies = load_tables(tables_hbm, tables, table_sems)
 
@@ -404,23 +421,14 @@
 
     for copy in table_copies:
         copy.wait()
-    loads[0].wait()
+    for load in loads[0:4]:
+        load.wait()
     scatter_rows(tables, fresh_ref, bricks_ref, 0, split, streams=streams, spans=spans, slot=slot)
-    loads[1].wait()
-
-    zeros = jnp.zeros((chans, size_y + 16, LANES), jnp.float32)
-    for x in (0, 1, size_x + 2, size_x + 3):
-        now_ref[:, x] = zeros
-    rim = jnp.zeros((8, LANES), jnp.float32)
-
-    @pl.loop(0, size_x // 2)
-    def _(bx):
-        for c in range(chans):
-            for dx in range(2):
-                now_ref[c, 2 * bx + dx + 2, 0:8, :] = rim
-                for y in range(0, size_y, 8):
-                    now_ref[c, 2 * bx + dx + 2, 8 + y : 16 + y, :] = cells(bricks_ref, c, dx, bx * half_y + y // 2)
-                now_ref[c, 2 * bx + dx + 2, size_y + 8 : size_y + 16, :] = rim
+    for load in loads[4:8]:
+        load.wait()
+
+    for bx, tiles in outer_tiles(size_x, size_y):
+        lay_out(bricks_ref, now_ref, bx, tiles)
 
     for side, add_ref in zip(stream_sides(), (first_add_ref, second_add_ref)):
         contribute(now_ref, jac_ref, side, add_ref)
@@ -458,16 +466,25 @@
 
 
 def edge_kernel(
-    tables_hbm, jac_ref, now_ref, bricks_in, fresh_ref, first_mine_ref, second_mine_ref,
-    bricks_ref, first_ref, second_ref, pre_ref, first_rim_ref, second_rim_ref,
+    tables_hbm, jac_ref, now_in, bricks_in, fresh_ref, first_mine_ref, second_mine_ref,
+    bricks_ref, now_ref, first_ref, second_ref, pre_ref, first_rim_ref, second_rim_ref,
     slope_ref, columns_ref, shifts_ref, table_sems,
     *, streams, spans, slot
 ):
-    del bricks_in
+    del bricks_in, now_in
     tables = (columns_ref, shifts_ref)
     copies = load_tables(tables_hbm, tables, table_sems)
     chans, size_x, size_y = now_ref.shape[0], now_ref.shape[1] - 4, now_ref.shape[2] - 16
     last = size_x - 1
+    for x in (0, 1, size_x + 2, size_x + 3):
+        now_ref[:, x] = jnp.zeros((chans, size_y + 16, LANES), jnp.float32)
+    rim = jnp.zeros((chans, 8, LANES), jnp.float32)
+    for x in range(2, size_x + 2):
+        now_ref[:, x, 0:8] = rim
+        now_ref[:, x, size_y + 8 : size_y + 16] = rim
+    done = dict(outer_tiles(size_x, size_y))
+    for bx in range(size_x // 2):
+        lay_out(bricks_ref, now_ref, bx, [y for y in range(0, size_y, 8) if y not in done.get(bx, [])])
     slope_planes(now_ref, slope_ref, 0, size_x)
     for copy in copies:
         copy.wait()
@@ -718,7 +735,7 @@
             pltpu.SMEM((1, slots), jnp.int32),
             pltpu.SMEM((1, slots), jnp.int32),
             pltpu.SemaphoreType.DMA((2,)),
-            pltpu.SemaphoreType.DMA((2,)),
+            pltpu.SemaphoreType.DMA((8,)),
         ],
         compiler_params=params(),
     )(tables, fractions.reshape(frac_rows, LANES // 2), jac, base, near)
@@ -732,20 +749,20 @@
     second_add = lax.ppermute(second_mine, "stream", along_stream[1])
     side = shape((5, chans, size_y, LANES), f32)
     rim = shape((size_x + 3, chans, 8, LANES), f32)
-    _, first, second, pre, first_rim, second_rim = pl.pallas_call(
+    _, _, first, second, pre, first_rim, second_rim = pl.pallas_call(
         functools.partial(edge_kernel, streams=streams, spans=spans, slot=slot),
         out_shape=[
-            shape(bricks.shape, f32), side, side, shape((chans, size_x - 10, size_y, LANES), f32), rim, rim
+            shape(bricks.shape, f32), shape(now.shape, f32), side, side, shape((chans, size_x - 10, size_y, LANES), f32), rim, rim
         ],
         in_specs=[HBM, SMEM] + [VMEM] * 5,
-        out_specs=[VMEM] * 6,
+        out_specs=[VMEM] * 7,
         scratch_shapes=[
             pltpu.VMEM((chans, size_x, size_y, LANES), f32),
             pltpu.SMEM((1, slots), jnp.int32),
             pltpu.SMEM((1, slots), jnp.int32),
             pltpu.SemaphoreType.DMA((2,)),
         ],
-        input_output_aliases={3: 0},
+        input_output_aliases={3: 0, 2: 1},
         compiler_params=params(),
     )(tables, jac, now, bricks, fresh, first_mine, second_mine)
     second = pl.pallas_call(

time: 62 us -> 61.7 us (level)
  no operation moved by 1% of the time
where the time goes in v3:
time: 61.7 us; the launch traced here: 61.4 us
  waiting for transfers between devices  24.6 us (40%)
  Pallas kernels  21.3 us (35%)
  starting transfers between devices  15.3 us (25%)
    all_to_all x1, waiting for transfers between devices, per_device(): lax.all_to_all(near, ('stream', 'span'), split_axis=0, concat_axis=0, til...  11.8 us
    ppermute x1, waiting for transfers between devices, per_device(): first_from = lax.ppermute(first, 'stream', along_stream[0])  11.7 us
    all_to_all x1, starting transfers between devices, per_device(): lax.all_to_all(near, ('stream', 'span'), split_axis=0, concat_axis=0, til...  7.42 us
    pallas_call x1, Pallas kernels, per_device(): pl.pallas_call(functools.partial(edge_kernel, streams=streams, spans=span...  5.96 us
    pallas_call x1, Pallas kernels, per_device(): pl.pallas_call(functools.partial(gather_kernel, streams=streams, spans=sp...  5.76 us
    pallas_call x1, Pallas kernels, per_device(): pl.pallas_call(functools.partial(fill_kernel, streams=streams, spans=span...  5.55 us
    ppermute x1, starting transfers between devices, per_device(): first_from = lax.ppermute(first, 'stream', along_stream[0])  4.36 us
    pallas_call x1, Pallas kernels, per_device(): pl.pallas_call(functools.partial(near_filter_kernel, spans=spans), out_sh...  2.78 us
  transfers between devices with their start and end apart: 7, of which 3 were waited for; matrix products, arithmetic and copies ran while one was open for 0% of the time, Pallas kernels for 14%

profile of v3, /device:TPU:0, one launch (start us, length us, event | category | flops | bytes accessed | tf_op | source)
XLA Modules:
  0.0 61.4 jit_solution(8635895445527597652)
XLA Ops:
  0.0 0.0 copy-start
  0.0 0.0 copy-start.1
  0.0 5.8 %shard_map.64 = (f32[1462,56,128]{2,1,0:T(8,128)}, f32[32,5,4,128]{3,2,1,0:T(4,128)}, s32[10240,1,1024]{2,1,0:T(1,128)}) custom-call(s32[1,1024]{1,0:T(1,128)} %send_hbm.1, s32[1,1024]{1,0:T(1,128)} %recv_hbm.1, f32[5,16,32,128]{3,2,1,0:T(8,128)} %now_hbm.1, f32[5,16,32,128]{3,2,1,0:T(8,128)} %old_hbm.1), custom_call_target="tpu_custom_call" | custom-call | tf_op jit(solution)/shard_map/pallas_call | solution.py:696
  5.8 7.4 %all-to-all-start = ((f32[32,5,4,128]{3,2,1,0:T(4,128)}), f32[32,5,4,128]{3,2,1,0:T(4,128)S(1)}, u32[]{:S(2)}, u32[]{:S(2)}) async-start(f32[32,5,4,128]{3,2,1,0:T(4,128)} %get-tuple-element.25), calls=%async_computation | async-start | bytes 655360 | tf_op jit(solution)/shard_map/all_to_all | solution.py:720
  13.2 0.0 copy-done
  13.3 0.1 reshape.3.frac_ref
  13.3 0.0 copy-done.1
  13.3 11.8 %all-to-all-done.near_ref = f32[32,5,4,128]{3,2,1,0:T(4,128)S(1)} async-done(((f32[32,5,4,128]{3,2,1,0:T(4,128)}), f32[32,5,4,128]{3,2,1,0:T(4,128)S(1)}, u32[]{:S(2)}, u32[]{:S(2)}) %all-to-all-start) | async-done | bytes 327712 | tf_op jit(solution)/shard_map/all_to_all | solution.py:720
  25.2 5.6 %shard_map.65 = (f32[129,56,128]{2,1,0:T(8,128)S(1)}, f32[11,40,128]{2,1,0:T(8,128)S(1)}, f32[5,20,48,128]{3,2,1,0:T(8,128)S(1)}, f32[5,88,128]{2,1,0:T(8,128)S(1)}, f32[5,88,128]{2,1,0:T(8,128)S(1)}) custom-call(s32[10240,1,1024]{2,1,0:T(1,128)} %get-tuple-element.23.tables_hbm, f32[48,64]{1,0:T(8,128)S(1)} %reshape.3.frac_ref, ...), custom_call_target="tpu_custom_call" | custom-call | tf_op jit(solution)/shard_map/pallas_call | solution.py:725
  30.8 1.4 %collective-permute-start = (f32[5,88,128]{2,1,0:T(8,128)S(1)}, f32[5,88,128]{2,1,0:T(8,128)S(1)}, u32[]{:S(2)}, u32[]{:S(2)}) collective-permute-start(f32[5,88,128]{2,1,0:T(8,128)S(1)} %get-tuple-element.29.first_mine_ref), channel_id=1, source_target_pairs={{0,4},{8,12},{16,20},{24,28},{4,0},{12,8},{20,16},{28,24},{1,5},{9... | collective-permute-start | bytes 675848 | tf_op jit(solution)/shard_map/ppermute | solution.py:748
  32.2 0.7 %collective-permute-start.1 = (f32[5,88,128]{2,1,0:T(8,128)S(1)}, f32[5,88,128]{2,1,0:T(8,128)S(1)}, u32[]{:S(2)}, u32[]{:S(2)}) collective-permute-start(f32[5,88,128]{2,1,0:T(8,128)S(1)} %get-tuple-element.30.second_mine_ref), channel_id=1, source_target_pairs={{4,8},{12,16},{20,24},{8,4},{16,12},{24,20},{5,9},{13,17},{21,25},... | collective-permute-start | bytes 675848 | tf_op jit(solution)/shard_map/ppermute | solution.py:749
  32.9 6.0 %shard_map.66 = (f32[129,56,128]{2,1,0:T(8,128)S(1)}, f32[5,20,48,128]{3,2,1,0:T(8,128)S(1)}, f32[5,5,32,128]{3,2,1,0:T(8,128)S(1)}, f32[5,5,32,128]{3,2,1,0:T(8...) custom-call(s32[10240,1,1024]{2,1,0:T(1,128)} %get-tuple-element.23., ...), custom_call_target="tpu_custom_call", output_to_operand_aliasing={{0}: (3, {}), {1}: (2, {})} | custom-call | tf_op jit(solution)/shard_map/pallas_call | solution.py:752
  38.8 4.4 %collective-permute-start.4 = (f32[5,5,32,128]{3,2,1,0:T(8,128)S(1)}, f32[5,5,32,128]{3,2,1,0:T(8,128)S(1)}, u32[]{:S(2)}, u32[]{:S(2)}) collective-permute-start(f32[5,5,32,128]{3,2,1,0:T(8,128)S(1)} %get-tuple-element.32.first_ref), channel_id=1, source_target_pairs={{0,4},{8,12},{16,20},{24,28},{4,0},{12,8},{20,16},{28,24},{1,5},{9... | collective-permute-start | bytes 1228808 | tf_op jit(solution)/shard_map/ppermute | solution.py:776
  43.2 0.0 collective-permute-done.add_ref.first_add_ref
  43.2 0.7 %collective-permute-start.5 = (f32[5,5,32,128]{3,2,1,0:T(8,128)S(1)}, f32[5,5,32,128]{3,2,1,0:T(8,128)S(1)}, u32[]{:S(2)}, u32[]{:S(2)}) collective-permute-start(f32[5,5,32,128]{3,2,1,0:T(8,128)S(1)} %shard_map.67.second_ref), channel_id=1, source_target_pairs={{4,8},{12,16},{20,24},{8,4},{16,12},{24,20},{5,9},{13,17},{21,25},... | collective-permute-start | bytes 1228808 | tf_op jit(solution)/shard_map/ppermute | solution.py:777
  43.9 0.0 collective-permute-done.1.second_add_ref
  43.9 0.1 shard_map.68
  44.0 0.1 collective-permute-start.2
  44.0 0.7 %collective-permute-start.3 = (f32[19,5,8,128]{3,2,1,0:T(8,128)S(1)}, f32[19,5,8,128]{3,2,1,0:T(8,128)S(1)}, u32[]{:S(2)}, u32[]{:S(2)}) collective-permute-start(f32[19,5,8,128]{3,2,1,0:T(8,128)S(1)} %get-tuple-element.37.second_rim_ref), channel_id=1, source_target_pairs={{1,2},{2,1},{5,6},{6,5},{9,10},{10,9},{13,14},{14,13},{17,18},{18,... | collective-permute-start | bytes 1167368 | tf_op jit(solution)/shard_map/ppermute | solution.py:787
  44.7 1.0 %collective-permute-done.2.first_from_ref = f32[19,5,8,128]{3,2,1,0:T(8,128)S(1)} collective-permute-done((f32[19,5,8,128]{3,2,1,0:T(8,128)S(1)}, f32[19,5,8,128]{3,2,1,0:T(8,128)S(1)}, u32[]{:S(2)}, u32[]{:S(2)}) %collective-permute-start.2) | collective-permute-done | bytes 389152 | tf_op jit(solution)/shard_map/ppermute | solution.py:786
  45.8 0.0 collective-permute-done.3.second_from_ref
  45.8 2.8 %shard_map.69 = (f32[5,16,32,128]{3,2,1,0:T(8,128)S(1)}, f32[3,5,8,128]{3,2,1,0:T(8,128)S(1)}, f32[3,5,8,128]{3,2,1,0:T(8,128)S(1)}) custom-call(f32[5,6,32,128]{3,2,1,0:T(8,128)S(1)} %get-tuple-element.31.pre_ref, f32[5,5,32,128]{3,2,1,0:T(8,128)S(1)} %get-tuple-element.32.first_ref, f32[5,5,32,128]{3,2,1,0:T(8,128)S(1)} %shard_map.67.second_ref, ...), custom_call_target="tpu_custom_call" | custom-call | tf_op jit(solution)/shard_map/pallas_call | solution.py:789
  48.5 11.7 %collective-permute-done.4.first_from_ref = f32[5,5,32,128]{3,2,1,0:T(8,128)S(1)} collective-permute-done((f32[5,5,32,128]{3,2,1,0:T(8,128)S(1)}, f32[5,5,32,128]{3,2,1,0:T(8,128)S(1)}, u32[]{:S(2)}, u32[]{:S(2)}) %collective-permute-start.4) | collective-permute-done | bytes 409632 | tf_op jit(solution)/shard_map/ppermute | solution.py:776
  60.2 0.0 collective-permute-done.5.second_from_ref
  60.2 1.1 %shard_map.70 = f32[5,16,32,128]{3,2,1,0:T(8,128)} custom-call(f32[5,16,32,128]{3,2,1,0:T(8,128)S(1)} %get-tuple-element.38.part_ref, f32[5,88,128]{2,1,0:T(8,128)S(1)} %get-tuple-element.29.first_mine_ref, f32[5,88,128]{2,1,0:T(8,128)S(1)} %get-tuple-element.30.second_mine_ref, f32[5,5,32,128]{3,2,1,0:T(8,128)S(1)} %collective-permute-done.4.first_from_ref, ...), custom_call_target="tpu_custom_call" | custom-call | tf_op jit(solution)/shard_map/pallas_call | solution.py:800
  (3 shorter events, 0.0 us)
Async XLA Ops:
  0.0 13.2 %copy-start = (f32[3,1,1024]{2,1,0:T(1,128)S(1)}, f32[3,1,1024]{2,1,0:T(1,128)}, u32[]{:S(2)}) copy-start(f32[3,1,1024]{2,1,0:T(1,128)} %param.9) | copy-start | bytes 36868
  0.0 13.3 %copy-start.1 = (f32[3,5,5]{2,0,1:T(4,128)S(1)}, f32[3,5,5]{2,0,1:T(4,128)}, u32[]{:S(2)}) copy-start(f32[3,5,5]{2,0,1:T(4,128)} %param.8) | copy-start | bytes 904
  5.8 19.4 %all-to-all-start = ((f32[32,5,4,128]{3,2,1,0:T(4,128)}), f32[32,5,4,128]{3,2,1,0:T(4,128)S(1)}, u32[]{:S(2)}, u32[]{:S(2)}) async-start(f32[32,5,4,128]{3,2,1,0:T(4,128)} %get-tuple-element.25), calls=%async_computation | async-start | bytes 655360 | tf_op jit(solution)/shard_map/all_to_all | solution.py:720
  30.8 12.4 %collective-permute-start = (f32[5,88,128]{2,1,0:T(8,128)S(1)}, f32[5,88,128]{2,1,0:T(8,128)S(1)}, u32[]{:S(2)}, u32[]{:S(2)}) collective-permute-start(f32[5,88,128]{2,1,0:T(8,128)S(1)} %get-tuple-element.29.first_mine_ref), channel_id=1, source_target_pairs={{0,4},{8,12},{16,20},{24,28},{4,0},{12,8},{20,16},{28,24},{1,5},{9... | collective-permute-start | bytes 675848 | tf_op jit(solution)/shard_map/ppermute | solution.py:748
  32.2 11.7 %collective-permute-start.1 = (f32[5,88,128]{2,1,0:T(8,128)S(1)}, f32[5,88,128]{2,1,0:T(8,128)S(1)}, u32[]{:S(2)}, u32[]{:S(2)}) collective-permute-start(f32[5,88,128]{2,1,0:T(8,128)S(1)} %get-tuple-element.30.second_mine_ref), channel_id=1, source_target_pairs={{4,8},{12,16},{20,24},{8,4},{16,12},{24,20},{5,9},{13,17},{21,25},... | collective-permute-start | bytes 675848 | tf_op jit(solution)/shard_map/ppermute | solution.py:749
  38.8 21.4 %collective-permute-start.4 = (f32[5,5,32,128]{3,2,1,0:T(8,128)S(1)}, f32[5,5,32,128]{3,2,1,0:T(8,128)S(1)}, u32[]{:S(2)}, u32[]{:S(2)}) collective-permute-start(f32[5,5,32,128]{3,2,1,0:T(8,128)S(1)} %get-tuple-element.32.first_ref), channel_id=1, source_target_pairs={{0,4},{8,12},{16,20},{24,28},{4,0},{12,8},{20,16},{28,24},{1,5},{9... | collective-permute-start | bytes 1228808 | tf_op jit(solution)/shard_map/ppermute | solution.py:776
  43.2 17.0 %collective-permute-start.5 = (f32[5,5,32,128]{3,2,1,0:T(8,128)S(1)}, f32[5,5,32,128]{3,2,1,0:T(8,128)S(1)}, u32[]{:S(2)}, u32[]{:S(2)}) collective-permute-start(f32[5,5,32,128]{3,2,1,0:T(8,128)S(1)} %shard_map.67.second_ref), channel_id=1, source_target_pairs={{4,8},{12,16},{20,24},{8,4},{16,12},{24,20},{5,9},{13,17},{21,25},... | collective-permute-start | bytes 1228808 | tf_op jit(solution)/shard_map/ppermute | solution.py:777
  44.0 1.8 %collective-permute-start.2 = (f32[19,5,8,128]{3,2,1,0:T(8,128)S(1)}, f32[19,5,8,128]{3,2,1,0:T(8,128)S(1)}, u32[]{:S(2)}, u32[]{:S(2)}) collective-permute-start(f32[19,5,8,128]{3,2,1,0:T(8,128)S(1)} %get-tuple-element.36.first_rim_ref), channel_id=1, source_target_pairs={{0,1},{2,3},{1,0},{3,2},{4,5},{6,7},{5,4},{7,6},{8,9},{10,11},{9,8... | collective-permute-start | bytes 1167368 | tf_op jit(solution)/shard_map/ppermute | solution.py:786
  44.0 1.7 %collective-permute-start.3 = (f32[19,5,8,128]{3,2,1,0:T(8,128)S(1)}, f32[19,5,8,128]{3,2,1,0:T(8,128)S(1)}, u32[]{:S(2)}, u32[]{:S(2)}) collective-permute-start(f32[19,5,8,128]{3,2,1,0:T(8,128)S(1)} %get-tuple-element.37.second_rim_ref), channel_id=1, source_target_pairs={{1,2},{2,1},{5,6},{6,5},{9,10},{10,9},{13,14},{14,13},{17,18},{18,... | collective-permute-start | bytes 1167368 | tf_op jit(solution)/shard_map/ppermute | solution.py:787

commit v4 on v3

--- a/solution.py
+++ b/solution.py
@@ -45,10 +45,14 @@
     return first, second, third, fourth
 
 
+def turn(rank, ranks):
+    return lax.rem(rank + 1, ranks)
+
+
 def gather_kernel(
     send_hbm, recv_hbm, now_hbm, old_hbm, bricks_hbm, near_hbm, tables_hbm,
     fields_ref, bricks_ref, near_ref, turned_ref, stage_ref, send_ref, recv_ref, spot_ref, spots_ref, shelves_ref,
-    load_sems, brick_sem, near_sems, table_sems,
+    load_sems, brick_sems, near_sems, table_sems,
     *, streams, spans, slot
 ):
     chans, size_x, size_y, size_z = now_hbm.shape
@@ -57,6 +61,7 @@
     rows = 8 * chans
     columns = size_x // 2 * half_y
     here, across = lax.axis_index("stream"), lax.axis_index("span")
+    ranks_all = streams * spans
 
     def chunk(n, bx):
         src = (now_hbm, old_hbm)[n].at[:, pl.ds(2 * bx, 2)]
@@ -110,14 +115,15 @@
                     part = fields_ref[c, 2 * bx + dx, start : start + 8, :]
                     total = part if total is None else jnp.where(quarter == t, part, total)
                 bricks_ref[bx * half_y + by + 1, 8 * v + 8 : 8 * v + 16, :] = total
+        inner = (pl.ds(1 + bx * half_y, half_y), pl.ds(8, rows))
+        kept.append(pltpu.make_async_copy(bricks_ref.at[inner], bricks_hbm.at[inner], brick_sems.at[bx]))
+        kept[-1].start()
         ready = (bx + 1) * half_y
         while 3 * turned < columns and min(3 * turned + 3, columns) <= ready:
             parts = [bricks_ref[min(3 * turned + r + 1, columns), 8 : 8 + rows, :] for r in range(3)]
             turned_ref[turned * LANES : (turned + 1) * LANES, :] = jnp.concatenate([*parts, blank], 0).T
             turned += 1
 
-    keep = pltpu.make_async_copy(bricks_ref, bricks_hbm.at[pl.ds(0, columns + 1)], brick_sem)
-    keep.start()
 
     for copy in tables:
         copy.wait()
@@ -141,11 +147,11 @@
                 parts.append(jnp.where(lane < rows, even, odd))
             for q, part in enumerate(pack_records(parts)):
                 near_ref[rank, q] = part
-            pltpu.make_async_copy(near_ref.at[rank], near_hbm.at[rank], near_sems.at[rank]).start()
+            pltpu.make_async_copy(near_ref.at[rank], near_hbm.at[turn(rank, ranks_all)], near_sems.at[rank]).start()
 
     def finish(ranks):
         for rank in ranks:
-            pltpu.make_async_copy(near_ref.at[rank], near_hbm.at[rank], near_sems.at[rank]).wait()
+            pltpu.make_async_copy(near_ref.at[rank], near_hbm.at[turn(rank, ranks_all)], near_sems.at[rank]).wait()
 
     opposite = lax.rem(here + streams // 2, streams) * spans + across
     per_offset = spans // 2
@@ -174,7 +180,6 @@
             finish(ranks)
 
     finish((opposite,))
-    keep.wait()
     for copy in kept:
         copy.wait()
 
@@ -378,7 +383,7 @@
         for h in range(2):
             blocks = []
             for _, rank, count, _ in members:
-                packed = [near_ref[rank + min(h, count - 1), q] for q in range(5)]
+                packed = [near_ref[turn(rank + min(h, count - 1), 2 * ranks), q] for q in range(5)]
                 blocks.append(unpack_records(packed))
             while len(blocks) < 3:
                 blocks.append(blocks[-1])
@@ -710,14 +715,17 @@
             pltpu.SMEM((1, slots), jnp.int32),
             pltpu.SMEM((1, slots), jnp.int32),
             pltpu.SemaphoreType.DMA((2, size_x // 2)),
-            pltpu.SemaphoreType.DMA,
+            pltpu.SemaphoreType.DMA((size_x // 2,)),
             pltpu.SemaphoreType.DMA((streams * spans,)),
             pltpu.SemaphoreType.DMA((6,)),
         ],
         compiler_params=params(BIG_VMEM_BYTES),
     )(send_blocks, recv_blocks, q_now, q_prev)
 
-    near = lax.all_to_all(near, ("stream", "span"), split_axis=0, concat_axis=0, tiled=True)
+    ranks = streams * spans
+    places = [[(place - 1) % ranks for place in range(ranks)]]
+    axes = ("stream", "span")
+    near = lax.all_to_all(near, axes, split_axis=0, concat_axis=0, tiled=True, axis_index_groups=places)
 
     jac = jacobians * (-1.0 / 36.0)
     frac_rows = 3 * streams * spans // 2

time: 61.7 us -> 61.7 us (level)
  no operation moved by 1% of the time
where the time goes in v4:
time: 61.7 us; the launch traced here: 61.4 us
  waiting for transfers between devices  24.5 us (40%)
  Pallas kernels  21.3 us (35%)
  starting transfers between devices  15.3 us (25%)
    all_to_all x1, waiting for transfers between devices, per_device(): lax.all_to_all(near, axes, split_axis=0, concat_axis=0, tiled=True, axis_...  11.8 us
    ppermute x1, waiting for transfers between devices, per_device(): first_from = lax.ppermute(first, 'stream', along_stream[0])  11.7 us
    all_to_all x1, starting transfers between devices, per_device(): lax.all_to_all(near, axes, split_axis=0, concat_axis=0, tiled=True, axis_...  7.42 us
    pallas_call x1, Pallas kernels, per_device(): pl.pallas_call(functools.partial(edge_kernel, streams=streams, spans=span...  5.96 us
    pallas_call x1, Pallas kernels, per_device(): pl.pallas_call(functools.partial(gather_kernel, streams=streams, spans=sp...  5.81 us
    pallas_call x1, Pallas kernels, per_device(): pl.pallas_call(functools.partial(fill_kernel, streams=streams, spans=span...  5.52 us
    ppermute x1, starting transfers between devices, per_device(): first_from = lax.ppermute(first, 'stream', along_stream[0])  4.36 us
    pallas_call x1, Pallas kernels, per_device(): pl.pallas_call(functools.partial(near_filter_kernel, spans=spans), out_sh...  2.78 us
  transfers between devices with their start and end apart: 7, of which 3 were waited for; matrix products, arithmetic and copies ran while one was open for 0% of the time, Pallas kernels for 14%

profile of v4, /device:TPU:0, one launch (start us, length us, event | category | flops | bytes accessed | tf_op | source)
XLA Modules:
  0.0 61.4 jit_solution(17683291010715616122)
XLA Ops:
  0.0 0.0 copy-start
  0.0 0.0 copy-start.1
  0.0 5.8 %shard_map.64 = (f32[1462,56,128]{2,1,0:T(8,128)}, f32[32,5,4,128]{3,2,1,0:T(4,128)}, s32[10240,1,1024]{2,1,0:T(1,128)}) custom-call(s32[1,1024]{1,0:T(1,128)} %send_hbm.1, s32[1,1024]{1,0:T(1,128)} %recv_hbm.1, f32[5,16,32,128]{3,2,1,0:T(8,128)} %now_hbm.1, f32[5,16,32,128]{3,2,1,0:T(8,128)} %old_hbm.1), custom_call_target="tpu_custom_call" | custom-call | tf_op jit(solution)/shard_map/pallas_call | solution.py:701
  5.8 7.4 %all-to-all-start = ((f32[32,5,4,128]{3,2,1,0:T(4,128)}), f32[32,5,4,128]{3,2,1,0:T(4,128)S(1)}, u32[]{:S(2)}, u32[]{:S(2)}) async-start(f32[32,5,4,128]{3,2,1,0:T(4,128)} %get-tuple-element.25), calls=%async_computation | async-start | bytes 655360 | tf_op jit(solution)/shard_map/all_to_all | solution.py:728
  13.3 0.0 copy-done
  13.3 0.1 reshape.3.frac_ref
  13.4 0.0 copy-done.1
  13.4 11.8 %all-to-all-done.near_ref = f32[32,5,4,128]{3,2,1,0:T(4,128)S(1)} async-done(((f32[32,5,4,128]{3,2,1,0:T(4,128)}), f32[32,5,4,128]{3,2,1,0:T(4,128)S(1)}, u32[]{:S(2)}, u32[]{:S(2)}) %all-to-all-start) | async-done | bytes 327712 | tf_op jit(solution)/shard_map/all_to_all | solution.py:728
  25.2 5.5 %shard_map.65 = (f32[129,56,128]{2,1,0:T(8,128)S(1)}, f32[11,40,128]{2,1,0:T(8,128)S(1)}, f32[5,20,48,128]{3,2,1,0:T(8,128)S(1)}, f32[5,88,128]{2,1,0:T(8,128)S(1)}, f32[5,88,128]{2,1,0:T(8,128)S(1)}) custom-call(s32[10240,1,1024]{2,1,0:T(1,128)} %get-tuple-element.23.tables_hbm, f32[48,64]{1,0:T(8,128)S(1)} %reshape.3.frac_ref, ...), custom_call_target="tpu_custom_call" | custom-call | tf_op jit(solution)/shard_map/pallas_call | solution.py:733
  30.8 1.4 %collective-permute-start = (f32[5,88,128]{2,1,0:T(8,128)S(1)}, f32[5,88,128]{2,1,0:T(8,128)S(1)}, u32[]{:S(2)}, u32[]{:S(2)}) collective-permute-start(f32[5,88,128]{2,1,0:T(8,128)S(1)} %get-tuple-element.29.first_mine_ref), channel_id=1, source_target_pairs={{0,4},{8,12},{16,20},{24,28},{4,0},{12,8},{20,16},{28,24},{1,5},{9... | collective-permute-start | bytes 675848 | tf_op jit(solution)/shard_map/ppermute | solution.py:756
  32.2 0.7 %collective-permute-start.1 = (f32[5,88,128]{2,1,0:T(8,128)S(1)}, f32[5,88,128]{2,1,0:T(8,128)S(1)}, u32[]{:S(2)}, u32[]{:S(2)}) collective-permute-start(f32[5,88,128]{2,1,0:T(8,128)S(1)} %get-tuple-element.30.second_mine_ref), channel_id=1, source_target_pairs={{4,8},{12,16},{20,24},{8,4},{16,12},{24,20},{5,9},{13,17},{21,25},... | collective-permute-start | bytes 675848 | tf_op jit(solution)/shard_map/ppermute | solution.py:757
  32.9 6.0 %shard_map.66 = (f32[129,56,128]{2,1,0:T(8,128)S(1)}, f32[5,20,48,128]{3,2,1,0:T(8,128)S(1)}, f32[5,5,32,128]{3,2,1,0:T(8,128)S(1)}, f32[5,5,32,128]{3,2,1,0:T(8...) custom-call(s32[10240,1,1024]{2,1,0:T(1,128)} %get-tuple-element.23., ...), custom_call_target="tpu_custom_call", output_to_operand_aliasing={{0}: (3, {}), {1}: (2, {})} | custom-call | tf_op jit(solution)/shard_map/pallas_call | solution.py:760
  38.9 4.4 %collective-permute-start.4 = (f32[5,5,32,128]{3,2,1,0:T(8,128)S(1)}, f32[5,5,32,128]{3,2,1,0:T(8,128)S(1)}, u32[]{:S(2)}, u32[]{:S(2)}) collective-permute-start(f32[5,5,32,128]{3,2,1,0:T(8,128)S(1)} %get-tuple-element.32.first_ref), channel_id=1, source_target_pairs={{0,4},{8,12},{16,20},{24,28},{4,0},{12,8},{20,16},{28,24},{1,5},{9... | collective-permute-start | bytes 1228808 | tf_op jit(solution)/shard_map/ppermute | solution.py:784
  43.2 0.0 collective-permute-done.add_ref.first_add_ref
  43.2 0.7 %collective-permute-start.5 = (f32[5,5,32,128]{3,2,1,0:T(8,128)S(1)}, f32[5,5,32,128]{3,2,1,0:T(8,128)S(1)}, u32[]{:S(2)}, u32[]{:S(2)}) collective-permute-start(f32[5,5,32,128]{3,2,1,0:T(8,128)S(1)} %shard_map.67.second_ref), channel_id=1, source_target_pairs={{4,8},{12,16},{20,24},{8,4},{16,12},{24,20},{5,9},{13,17},{21,25},... | collective-permute-start | bytes 1228808 | tf_op jit(solution)/shard_map/ppermute | solution.py:785
  43.9 0.0 collective-permute-done.1.second_add_ref
  43.9 0.1 shard_map.68
  44.0 0.1 collective-permute-start.2
  44.1 0.7 %collective-permute-start.3 = (f32[19,5,8,128]{3,2,1,0:T(8,128)S(1)}, f32[19,5,8,128]{3,2,1,0:T(8,128)S(1)}, u32[]{:S(2)}, u32[]{:S(2)}) collective-permute-start(f32[19,5,8,128]{3,2,1,0:T(8,128)S(1)} %get-tuple-element.37.second_rim_ref), channel_id=1, source_target_pairs={{1,2},{2,1},{5,6},{6,5},{9,10},{10,9},{13,14},{14,13},{17,18},{18,... | collective-permute-start | bytes 1167368 | tf_op jit(solution)/shard_map/ppermute | solution.py:795
  44.8 1.0 %collective-permute-done.2.first_from_ref = f32[19,5,8,128]{3,2,1,0:T(8,128)S(1)} collective-permute-done((f32[19,5,8,128]{3,2,1,0:T(8,128)S(1)}, f32[19,5,8,128]{3,2,1,0:T(8,128)S(1)}, u32[]{:S(2)}, u32[]{:S(2)}) %collective-permute-start.2) | collective-permute-done | bytes 389152 | tf_op jit(solution)/shard_map/ppermute | solution.py:794
  45.8 0.0 collective-permute-done.3.second_from_ref
  45.8 2.8 %shard_map.69 = (f32[5,16,32,128]{3,2,1,0:T(8,128)S(1)}, f32[3,5,8,128]{3,2,1,0:T(8,128)S(1)}, f32[3,5,8,128]{3,2,1,0:T(8,128)S(1)}) custom-call(f32[5,6,32,128]{3,2,1,0:T(8,128)S(1)} %get-tuple-element.31.pre_ref, f32[5,5,32,128]{3,2,1,0:T(8,128)S(1)} %get-tuple-element.32.first_ref, f32[5,5,32,128]{3,2,1,0:T(8,128)S(1)} %shard_map.67.second_ref, ...), custom_call_target="tpu_custom_call" | custom-call | tf_op jit(solution)/shard_map/pallas_call | solution.py:797
  48.6 11.7 %collective-permute-done.4.first_from_ref = f32[5,5,32,128]{3,2,1,0:T(8,128)S(1)} collective-permute-done((f32[5,5,32,128]{3,2,1,0:T(8,128)S(1)}, f32[5,5,32,128]{3,2,1,0:T(8,128)S(1)}, u32[]{:S(2)}, u32[]{:S(2)}) %collective-permute-start.4) | collective-permute-done | bytes 409632 | tf_op jit(solution)/shard_map/ppermute | solution.py:784
  60.2 0.0 collective-permute-done.5.second_from_ref
  60.2 1.1 %shard_map.70 = f32[5,16,32,128]{3,2,1,0:T(8,128)} custom-call(f32[5,16,32,128]{3,2,1,0:T(8,128)S(1)} %get-tuple-element.38.part_ref, f32[5,88,128]{2,1,0:T(8,128)S(1)} %get-tuple-element.29.first_mine_ref, f32[5,88,128]{2,1,0:T(8,128)S(1)} %get-tuple-element.30.second_mine_ref, f32[5,5,32,128]{3,2,1,0:T(8,128)S(1)} %collective-permute-done.4.first_from_ref, ...), custom_call_target="tpu_custom_call" | custom-call | tf_op jit(solution)/shard_map/pallas_call | solution.py:808
  (3 shorter events, 0.0 us)
Async XLA Ops:
  0.0 13.3 %copy-start = (f32[3,1,1024]{2,1,0:T(1,128)S(1)}, f32[3,1,1024]{2,1,0:T(1,128)}, u32[]{:S(2)}) copy-start(f32[3,1,1024]{2,1,0:T(1,128)} %param.9) | copy-start | bytes 36868
  0.0 13.4 %copy-start.1 = (f32[3,5,5]{2,0,1:T(4,128)S(1)}, f32[3,5,5]{2,0,1:T(4,128)}, u32[]{:S(2)}) copy-start(f32[3,5,5]{2,0,1:T(4,128)} %param.8) | copy-start | bytes 904
  5.8 19.4 %all-to-all-start = ((f32[32,5,4,128]{3,2,1,0:T(4,128)}), f32[32,5,4,128]{3,2,1,0:T(4,128)S(1)}, u32[]{:S(2)}, u32[]{:S(2)}) async-start(f32[32,5,4,128]{3,2,1,0:T(4,128)} %get-tuple-element.25), calls=%async_computation | async-start | bytes 655360 | tf_op jit(solution)/shard_map/all_to_all | solution.py:728
  30.8 12.4 %collective-permute-start = (f32[5,88,128]{2,1,0:T(8,128)S(1)}, f32[5,88,128]{2,1,0:T(8,128)S(1)}, u32[]{:S(2)}, u32[]{:S(2)}) collective-permute-start(f32[5,88,128]{2,1,0:T(8,128)S(1)} %get-tuple-element.29.first_mine_ref), channel_id=1, source_target_pairs={{0,4},{8,12},{16,20},{24,28},{4,0},{12,8},{20,16},{28,24},{1,5},{9... | collective-permute-start | bytes 675848 | tf_op jit(solution)/shard_map/ppermute | solution.py:756
  32.2 11.7 %collective-permute-start.1 = (f32[5,88,128]{2,1,0:T(8,128)S(1)}, f32[5,88,128]{2,1,0:T(8,128)S(1)}, u32[]{:S(2)}, u32[]{:S(2)}) collective-permute-start(f32[5,88,128]{2,1,0:T(8,128)S(1)} %get-tuple-element.30.second_mine_ref), channel_id=1, source_target_pairs={{4,8},{12,16},{20,24},{8,4},{16,12},{24,20},{5,9},{13,17},{21,25},... | collective-permute-start | bytes 675848 | tf_op jit(solution)/shard_map/ppermute | solution.py:757
  38.9 21.4 %collective-permute-start.4 = (f32[5,5,32,128]{3,2,1,0:T(8,128)S(1)}, f32[5,5,32,128]{3,2,1,0:T(8,128)S(1)}, u32[]{:S(2)}, u32[]{:S(2)}) collective-permute-start(f32[5,5,32,128]{3,2,1,0:T(8,128)S(1)} %get-tuple-element.32.first_ref), channel_id=1, source_target_pairs={{0,4},{8,12},{16,20},{24,28},{4,0},{12,8},{20,16},{28,24},{1,5},{9... | collective-permute-start | bytes 1228808 | tf_op jit(solution)/shard_map/ppermute | solution.py:784
  43.2 17.0 %collective-permute-start.5 = (f32[5,5,32,128]{3,2,1,0:T(8,128)S(1)}, f32[5,5,32,128]{3,2,1,0:T(8,128)S(1)}, u32[]{:S(2)}, u32[]{:S(2)}) collective-permute-start(f32[5,5,32,128]{3,2,1,0:T(8,128)S(1)} %shard_map.67.second_ref), channel_id=1, source_target_pairs={{4,8},{12,16},{20,24},{8,4},{16,12},{24,20},{5,9},{13,17},{21,25},... | collective-permute-start | bytes 1228808 | tf_op jit(solution)/shard_map/ppermute | solution.py:785
  44.0 1.8 %collective-permute-start.2 = (f32[19,5,8,128]{3,2,1,0:T(8,128)S(1)}, f32[19,5,8,128]{3,2,1,0:T(8,128)S(1)}, u32[]{:S(2)}, u32[]{:S(2)}) collective-permute-start(f32[19,5,8,128]{3,2,1,0:T(8,128)S(1)} %get-tuple-element.36.first_rim_ref), channel_id=1, source_target_pairs={{0,1},{2,3},{1,0},{3,2},{4,5},{6,7},{5,4},{7,6},{8,9},{10,11},{9,8... | collective-permute-start | bytes 1167368 | tf_op jit(solution)/shard_map/ppermute | solution.py:794
  44.1 1.7 %collective-permute-start.3 = (f32[19,5,8,128]{3,2,1,0:T(8,128)S(1)}, f32[19,5,8,128]{3,2,1,0:T(8,128)S(1)}, u32[]{:S(2)}, u32[]{:S(2)}) collective-permute-start(f32[19,5,8,128]{3,2,1,0:T(8,128)S(1)} %get-tuple-element.37.second_rim_ref), channel_id=1, source_target_pairs={{1,2},{2,1},{5,6},{6,5},{9,10},{10,9},{13,14},{14,13},{17,18},{18,... | collective-permute-start | bytes 1167368 | tf_op jit(solution)/shard_map/ppermute | solution.py:795
